TPU v7x, 256 devices: a whole 4x4x8 slice. The times are simulated.
256 devices in a mesh: pcol: 32 (over y, x, core), prow: 8 (over z).
Axes of the slice: x: 4, y: 4, z: 8, core: 2. Of those that a mesh axis runs over, the one named last changes fastest.
Arguments:
- matrix: float32 [8, 32, 48, 32768], P(None, 'pcol', None, 'prow'), may hold values from -6 to 6, as said below
- pivots: int32 [96], replicated, may hold values from 0 to 32767, as said below
Outputs:
- factored: float32 [8, 32, 48, 32768], P(None, 'pcol', None, 'prow')
Inputs may be any that keep to these rules, and one draw needn't show every extreme that they name: pivots[j] lies between j and 32767; some entry equals 32767. `matrix`: after the interchanges, the top 2 * 48 x 2 * 48 block of B is diagonally dominant by rows: diagonal entries of magnitude 4 to 6, off-diagonal magnitudes in a row summing to at most 3.5.
All inputs are finite; a program needn't handle non-finite values.
Results may differ from a plain program's by a relative error of at most 0.0001.
Values sent between devices are 32-bit elements; how exact they have to be, the bound alone decides.
No kernel may reach another device: no remote copies, remote signals or barrier semaphores. Data moves between devices by JAX's collectives and lax.ppermute only.
A program may use at most 64 MiB of HBM per device.

v0:
```python
import jax
import jax.numpy as jnp
from jax import lax
from jax.sharding import PartitionSpec as P


def broadcast(shard, axis, root):
    mine = lax.axis_index(axis) == root
    return lax.psum(jnp.where(mine, shard, jnp.zeros_like(shard)), axis)


def compose(swap_targets, length):
    ordering = jnp.arange(length, dtype=jnp.int32)

    def compose_advance(counter, current):
        target = swap_targets[counter]
        at_counter = current[counter]
        at_target = current[target]
        return current.at[counter].set(at_target).at[target].set(at_counter)

    return lax.fori_loop(0, swap_targets.shape[0], compose_advance, ordering)


def sweep_lower(coeffs, rhs, unit_diag):
    extent = coeffs.shape[0]
    indices = jnp.arange(extent)

    def sweep_advance(counter, current):
        head = current[counter]
        if not unit_diag:
            head = head / coeffs[counter, counter]
        current = current.at[counter].set(head)
        column = jnp.where(indices > counter, coeffs[:, counter], 0.0)
        return current - column[:, None] * head[None, :]

    return lax.fori_loop(0, extent, sweep_advance, rhs)


def eliminate(square):
    extent = square.shape[0]
    indices = jnp.arange(extent)

    def eliminate_advance(counter, current):
        pivot_row = current[counter]
        column = current[:, counter] / pivot_row[counter]
        beneath = indices > counter
        current = (
            current
            - jnp.where(beneath, column, 0.0)[:, None] * jnp.where(beneath, pivot_row, 0.0)[None, :]
        )
        return jnp.where(beneath[:, None] & (indices[None, :] == counter), column[:, None], current)

    return lax.fori_loop(0, extent, eliminate_advance, square)


def factor_panel(raw_lower, raw_top, begin_col):
    panel_width = raw_lower.shape[0]
    finish_col = begin_col + panel_width
    factored = eliminate(raw_top[:, begin_col:finish_col].T)
    upper_part = jnp.triu(factored)
    lower_rows = sweep_lower(upper_part.T, raw_lower, False)
    top_solved = sweep_lower(upper_part.T, raw_top, False)
    positions = jnp.arange(raw_top.shape[1])
    done_top = jnp.where((positions >= finish_col)[None, :], top_solved, raw_top)
    done_top = done_top.at[:, begin_col:finish_col].set(factored.T)
    return (lower_rows, done_top)


def apply_panel(columns_low, columns_top, lower_rows, done_top, begin_col, selected):
    panel_width = lower_rows.shape[0]
    finish_col = begin_col + panel_width
    unit_lower = jnp.tril(done_top[:, begin_col:finish_col].T, -1) + jnp.eye(
        panel_width, dtype=jnp.float32
    )
    solved = sweep_lower(unit_lower, columns_top[:, begin_col:finish_col].T, True)
    positions = jnp.arange(done_top.shape[1])
    top_factors = jnp.where((positions >= finish_col)[None, :], done_top, 0.0)
    new_low = columns_low - jnp.dot(
        solved.T, lower_rows, precision=lax.Precision.HIGHEST, preferred_element_type=jnp.float32
    )
    new_top = columns_top - jnp.dot(
        solved.T, top_factors, precision=lax.Precision.HIGHEST, preferred_element_type=jnp.float32
    )
    new_top = new_top.at[:, begin_col:finish_col].set(solved.T)
    return (
        jnp.where(selected[:, None], new_low, columns_low),
        jnp.where(selected[:, None], new_top, columns_top),
    )


def place_panel(columns_low, columns_top, lower_rows, done_top, owner):
    panel_width = lower_rows.shape[0]
    columns_low = columns_low.at[:panel_width].set(
        jnp.where(owner, lower_rows, columns_low[:panel_width])
    )
    columns_top = columns_top.at[:panel_width].set(
        jnp.where(owner, done_top, columns_top[:panel_width])
    )
    return (columns_low, columns_top)


def on_device(matrix, pivots):
    blocks_here, _, panel_width, row_count = matrix.shape
    top_span = 2 * panel_width
    holdings = matrix.reshape(blocks_here * panel_width, row_count)
    row_base = lax.axis_index("prow") * row_count
    column_rank = lax.axis_index("pcol")
    total_rows = row_count * lax.axis_size("prow")
    ordering = compose(pivots, total_rows)
    wanted = ordering[:top_span]
    owned_rows = (wanted >= row_base) & (wanted < row_base + row_count)
    picked = jnp.take(holdings, jnp.clip(wanted - row_base, 0, row_count - 1), axis=1)
    offered = jnp.where(owned_rows[None, :], picked, 0.0)
    top_rows = lax.psum(offered, "prow")
    starting_rows = broadcast(holdings[:, :top_span], "prow", 0)
    inverse_order = (
        jnp.zeros((total_rows,), jnp.int32)
        .at[ordering]
        .set(jnp.arange(total_rows, dtype=jnp.int32))
    )
    destinations = inverse_order[:top_span]
    local_dest = destinations - row_base
    usable = (destinations >= top_span) & (local_dest >= 0) & (local_dest < row_count)
    local_dest = jnp.where(usable, local_dest, row_count)
    holdings = holdings.at[:, local_dest].set(starting_rows, mode="drop")
    block_ids = (
        jnp.arange(blocks_here * panel_width) // panel_width * lax.axis_size("pcol") + column_rank
    )
    lower_one, top_one = factor_panel(holdings[:panel_width], top_rows[:panel_width], 0)
    lower_one, top_one = (broadcast(lower_one, "pcol", 0), broadcast(top_one, "pcol", 0))
    holdings, top_rows = apply_panel(holdings, top_rows, lower_one, top_one, 0, block_ids > 0)
    holdings, top_rows = place_panel(holdings, top_rows, lower_one, top_one, column_rank == 0)
    lower_two, top_two = factor_panel(holdings[:panel_width], top_rows[:panel_width], panel_width)
    lower_two, top_two = (broadcast(lower_two, "pcol", 1), broadcast(top_two, "pcol", 1))
    holdings, top_rows = apply_panel(
        holdings, top_rows, lower_two, top_two, panel_width, block_ids > 1
    )
    holdings, top_rows = place_panel(holdings, top_rows, lower_two, top_two, column_rank == 1)
    head_block = jnp.where(row_base == 0, top_rows, holdings[:, :top_span])
    result = holdings.at[:, :top_span].set(head_block)
    return result.reshape(matrix.shape)


def solution(mesh):
    placed = (P(None, "pcol", None, "prow"), P())
    return jax.shard_map(
        on_device,
        mesh=mesh,
        in_specs=placed,
        out_specs=P(None, "pcol", None, "prow"),
        check_vma=False,
    )
```

profile of v0, /device:TPU:1, one launch (start us, length us, event | category | flops | bytes accessed | tf_op | source)
XLA Modules:
  0.0 1964.1 jit_solution(16787829730235970664)
XLA Ops:
  6.6 559.4 %while.150 = (s32[]{:T(128)}, s32[32768]{0:T(1024)S(1)}, s32[96]{0:T(128)}, s32[]{:T(128)}, s32[]{:T(128)}, /*index=5*/s32[]{:T(128)}, s32[]{:T(128)}) while((s32[]{:T(128)}, s32[32768]{0:T(1024)S(1)}, s32[96]{0:T(128)}, s32[]{:T(128)}, s32[]{:T(128)}, /*index=5*/s32[]{:T(128)}, s32[]{:T(128)}) %tuple.410), condition=%wide.region_1.2_spmd, body=%wide.region_0.1_spmd.sunk | while | flops 13 | bytes 2247 | solution.py:21
  6.6 1.3 dynamic_slice.265
  12.4 1.3 dynamic_slice.265
  24.0 1.3 dynamic_slice.265
  35.7 1.3 dynamic_slice.265
  47.4 1.3 dynamic_slice.265
  64.8 1.3 dynamic_slice.265
  566.0 6.6 copy.23
  572.6 3.5 gather_fusion
  576.2 1.6 slice_select_fusion.3
  580.1 120.1 %scatter_custom_fusion = s32[32768]{0:T(1024)S(1)} fusion(s32[32768]{0:T(1024)S(1)} %compare_select_fusion, s32[32768]{0:T(1024)S(1)} %iota.132, s32[]{:T(128)} %constant.948.clone.1), kind=kCustom, calls=%fused_computation.81 | custom fusion | bytes 131076 | tf_op jit(solution)/shard_map/scatter | solution.py:119
  702.7 71.7 %while.157 = (s32[]{:T(128)}, f32[48,48]{0,1:T(8,128)S(1)}, s32[]{:T(128)}, s32[]{:T(128)}, s32[]{:T(128)}) while((s32[]{:T(128)}, f32[48,48]{0,1:T(8,128)S(1)}, s32[]{:T(128)}, s32[]{:T(128)}, s32[]{:T(128)}) %tuple.413), condition=%wide.region_7.8_spmd.clone.clone, body=%wide.region_6.7_spmd.clone.clone.sunk | while | flops 9555 | bytes 41245 | solution.py:53
  774.5 132.5 %while.151 = (s32[]{:T(128)}, f32[48,96]{1,0:T(8,128)S(1)}, f32[48,48]{0,1:T(8,128)S(1)}, s32[]{:T(128)}, s32[2]{0:T(128)S(1)}, /*index=5*/s32[1]{0:T(128)}, s32[]{:T(128)}) while((s32[]{:T(128)}, f32[48,96]{1,0:T(8,128)S(1)}, f32[48,48]{0,1:T(8,128)S(1)}, s32[]{:T(128)}, s32[2]{0:T(128)S(1)}, /*index=5*/s32[1]{0:T(128)}, ...), condition=%wide.region_10.11_spmd.clone, body=%wide.region_8.10_spmd.clone.sunk | while | flops 9515 | bytes 40887 | solution.py:36
  908.7 124.2 %psum.44 = f32[48,96]{1,0:T(8,128)S(1)} all-reduce(f32[48,96]{1,0:T(8,128)S(1)} %broadcast_select_fusion.9), channel_id=1, replica_groups=mesh['pcol'=32,'prow'=8] {'pcol'}, use_global_device_ids=true, to_apply=%region_12.13 | all-reduce | flops 4608 | bytes 36864 | tf_op jit(solution)/shard_map/psum | solution.py:9
  1033.1 9.8 while.152
  1042.9 1.4 convolution_subtract_fusion.1
  1047.1 71.7 %while.158 = (s32[]{:T(128)}, f32[48,48]{0,1:T(8,128)S(1)}, s32[]{:T(128)}, s32[]{:T(128)}, s32[]{:T(128)}) while((s32[]{:T(128)}, f32[48,48]{0,1:T(8,128)S(1)}, s32[]{:T(128)}, s32[]{:T(128)}, s32[]{:T(128)}) %tuple.425), condition=%wide.region_20.21_spmd.clone.clone, body=%wide.region_19.20_spmd.clone.clone.sunk | while | flops 9555 | bytes 41245 | solution.py:53
  1118.9 133.6 %while.154 = (s32[]{:T(128)}, f32[48,96]{1,0:T(8,128)S(1)}, f32[48,48]{0,1:T(8,128)S(1)}, s32[]{:T(128)}, s32[2]{0:T(128)S(1)}, /*index=5*/s32[1]{0:T(128)}, s32[]{:T(128)}) while((s32[]{:T(128)}, f32[48,96]{1,0:T(8,128)S(1)}, f32[48,48]{0,1:T(8,128)S(1)}, s32[]{:T(128)}, s32[2]{0:T(128)S(1)}, /*index=5*/s32[1]{0:T(128)}, ...), condition=%wide.region_23.24_spmd.clone, body=%wide.region_21.23_spmd.clone.sunk | while | flops 9515 | bytes 40887 | solution.py:36
  1252.9 123.8 %psum.46 = f32[48,96]{1,0:T(8,128)S(1)} all-reduce(f32[48,96]{1,0:T(8,128)S(1)} %broadcast_select_fusion.8), channel_id=1, replica_groups=mesh['pcol'=32,'prow'=8] {'pcol'}, use_global_device_ids=true, to_apply=%region_24.25 | all-reduce | flops 4608 | bytes 36864 | tf_op jit(solution)/shard_map/psum | solution.py:9
  1377.1 6.3 scatter_fusion
  1383.5 1.7 slice.427
  1385.8 157.0 %while.153 = (s32[]{:T(128)}, f32[48,4096]{1,0:T(8,128)S(1)}, f32[48,48]{0,1:T(8,128)S(1)}, s32[]{:T(128)}, s32[2]{0:T(128)S(1)}, /*index=5*/s32[1]{0:T(128)}, s32[]{:T(128)}) while((s32[]{:T(128)}, f32[48,4096]{1,0:T(8,128)S(1)}, f32[48,48]{0,1:T(8,128)S(1)}, s32[]{:T(128)}, s32[2]{0:T(128)S(1)}, /*index=5*/s32[1]{0:T(128)}, ...), condition=%wide.region_17.18_spmd.clone, body=%wide.region_15.17_spmd.clone.sunk | while | flops 401515 | bytes 1672887 | solution.py:36
  1544.0 9.8 while.155
  1553.8 6.6 copy.31
  1562.1 98.5 %all-reduce.5.cloned.1.call-done = f32[48,4096]{1,0:T(8,128)} async-done(((f32[48,4096]{1,0:T(8,128)}), f32[48,4096]{1,0:T(8,128)}) %all-reduce.5.cloned.1.call-update) | async-done | bytes 786448 | tf_op jit(solution)/shard_map/psum | solution.py:9
  1660.6 9.7 subtract_select_fusion.3
  1670.3 2.1 constant_dynamic-update-slice_fusion.1
  1672.4 157.2 %while.156 = (s32[]{:T(128)}, f32[48,4096]{1,0:T(8,128)S(1)}, f32[48,48]{0,1:T(8,128)S(1)}, s32[]{:T(128)}, s32[2]{0:T(128)S(1)}, /*index=5*/s32[1]{0:T(128)}, s32[]{:T(128)}) while((s32[]{:T(128)}, f32[48,4096]{1,0:T(8,128)S(1)}, f32[48,48]{0,1:T(8,128)S(1)}, s32[]{:T(128)}, s32[2]{0:T(128)S(1)}, /*index=5*/s32[1]{0:T(128)}, ...), condition=%wide.region_29.30_spmd.clone, body=%wide.region_27.29_spmd.clone.sunk | while | flops 401515 | bytes 1672887 | solution.py:36
  1830.7 113.5 %all-reduce.7.cloned.1.call-done = f32[48,4096]{1,0:T(8,128)} async-done(((f32[48,4096]{1,0:T(8,128)}), f32[48,4096]{1,0:T(8,128)}) %all-reduce.7.cloned.1.call-update) | async-done | bytes 786448 | tf_op jit(solution)/shard_map/psum | solution.py:9
  1944.2 8.1 subtract_select_fusion.2
  1952.5 2.7 copy-done
  1955.9 1.8 scatter.94
  (2558 shorter events, 1096.9 us)
Async XLA Ops:
  6.5 693.7 %all-reduce.9.cloned.1.call-start = ((), (), s32[]{:S(2)}) async-start(), calls=%async_computation.2 | async-start | bytes 786432 | tf_op jit(solution)/shard_map/psum | solution.py:9
  566.0 208.5 %copy-start.3 = (s32[2]{0:T(128)S(1)}, s32[2]{0:T(128)}, u32[]{:S(2)}) copy-start(s32[2]{0:T(128)} %constant.908.clone.2) | copy-start | bytes 28
  578.6 1082.0 %all-reduce.5.cloned.1.call-start = ((), (), s32[]{:S(2)}) async-start(), calls=%async_computation | async-start | bytes 1572864 | tf_op jit(solution)/shard_map/psum | solution.py:9
  700.2 676.8 %copy-start.4 = (f32[384,96]{1,0:T(8,128)S(1)}, f32[384,96]{1,0:T(8,128)}, u32[]{:S(2)}) copy-start(f32[384,96]{1,0:T(8,128)} %get-tuple-element.1208) | copy-start | bytes 442372
  1543.8 400.4 %all-reduce.7.cloned.1.call-start = ((), (), s32[]{:S(2)}) async-start(), calls=%async_computation.1 | async-start | bytes 1572864 | tf_op jit(solution)/shard_map/psum | solution.py:9
  1660.6 9.7 copy-start.2
  1944.2 8.1 copy-start.1
  1952.5 2.7 copy-start
Sparse Core Ops, SparseCore 0:
  578.7 72.3 all-reduce.8
  1543.9 116.6 all-reduce.4
  1830.7 113.4 all-reduce.6
where the time goes:
time: 1970 us; the launch traced here: 1960 us
  other arithmetic  679 us (34%)
  local copies, waits for them, and re-layouts  578 us (29%)
  blocking collectives  248 us (13%)
  loops' own time  214 us (11%)
  waiting for transfers between devices  212 us (11%)
  matrix products  19.7 us (1%)
    another operation x389, other arithmetic  396 us
    psum x2, blocking collectives, broadcast(): return lax.psum(jnp.where(mine, shard, jnp.zeros_like(shard)), axis)  248 us
    psum x3, waiting for transfers between devices, broadcast(): return lax.psum(jnp.where(mine, shard, jnp.zeros_like(shard)), axis)  212 us
    another operation x1, loops' own time, compose(): return lax.fori_loop(0, swap_targets.shape[0], compose_advance, ordering)  200 us
    scatter x192, other arithmetic, compose_advance(): return current.at[counter].set(at_target).at[target].set(at_counter)  169 us
    dynamic_slice x96, local copies, waits for them, and re-layouts, compose_advance(): target = swap_targets[counter]  126 us
    scatter x1, local copies, waits for them, and re-layouts, on_device(): inverse_order = jnp.zeros((total_rows,), jnp.int32).at[ordering].set(jnp....  120 us
    dynamic_slice x192, local copies, waits for them, and re-layouts, sweep_advance(): head = head / coeffs[counter, counter]  113 us
  transfers between devices with their start and end apart: 3, of which 2 were waited for; matrix products, arithmetic and copies ran while one was open for 7% of the time, Pallas kernels for 0%

commit v1 on v0

v1 whole, which is shorter than its diff:
```python
import jax
import jax.numpy as jnp
from jax import lax
from jax.experimental import pallas as pl
from jax.experimental.pallas import tpu as pltpu
from jax.sharding import Mesh
from jax.sharding import PartitionSpec as P

HI = lax.Precision.HIGHEST
LANES = 128
F32 = jnp.float32
BF16 = jnp.bfloat16


def iota(shape, dim):
    return lax.broadcasted_iota(jnp.int32, shape, dim)


def vmem_spec():
    return pl.BlockSpec(memory_space=pltpu.VMEM)


def smem_spec():
    return pl.BlockSpec(memory_space=pltpu.SMEM)


def params(mib=48):
    return pltpu.CompilerParams(vmem_limit_bytes=mib * 1024 * 1024)


def cost(us):
    return pl.CostEstimate(flops=0, bytes_accessed=int(us * 3.5e6), transcendentals=0)


def pick_rows(wanted, base, rows, block, out, top):
    lanes = iota((block.shape[0], LANES), 1)

    def step(i, carry):
        local = wanted[i] - base

        @pl.when((local >= 0) & (local < rows))
        def _():
            start = pl.multiple_of((local // LANES) * LANES, LANES)
            shift = (i + LANES - local % LANES) % LANES
            moved = pltpu.roll(block[:, pl.ds(start, LANES)], shift, 1)
            out[...] = jnp.where(lanes == i, moved, out[...])

        return carry

    out[...] = jnp.zeros(out.shape, F32)
    lax.fori_loop(0, top, step, 0)


def start_kernel(top, pivots, base, panel, blocks, wanted, dest, current, goes, picked):
    rows = panel.shape[1]
    groups = blocks.shape[0]
    width = rows // groups

    def fill(j, carry):
        current[pivots[j]] = pivots[j]
        goes[j] = -1
        return carry

    def fill_top(j, carry):
        current[j] = j
        return carry

    def swap(j, carry):
        t = pivots[j]
        a = current[j]
        b = current[t]
        wanted[j] = b
        current[t] = a
        goes[jnp.minimum(b, top)] = -1
        goes[a] = jnp.where(t >= top, t, -1)
        return carry

    def emit(j, carry):
        dest[pl.ds(j, 1), :] = jnp.full((1, LANES), goes[j], jnp.int32)
        return carry

    lax.fori_loop(0, top, fill, 0, unroll=8)
    lax.fori_loop(0, top, fill_top, 0, unroll=8)
    lax.fori_loop(0, top, swap, 0, unroll=8)
    dest[...] = jnp.full(dest.shape, -1, jnp.int32)
    lax.fori_loop(0, top, emit, 0, unroll=8)
    pick_rows(wanted, base[0], rows, panel, picked, top)
    lanes = iota(picked.shape, 1)
    heads = jnp.where((base[0] == 0) & (lanes < top), panel[:, :LANES], 0.0)
    for g in range(groups):
        blocks[g, :, :width] = panel[:, g * width : (g + 1) * width]
        blocks[g, :, width : width + LANES] = picked[...]
        blocks[g, :, width + LANES :] = heads


def own_kernel(top, base, wanted, block, *refs):
    outs, picked = refs[:-1], refs[-1]
    depth = len(outs)
    rows = block.shape[1]
    part = block.shape[0] // depth
    pick_rows(wanted, base[0], rows, block, picked, top)
    place = base[0] // rows
    for k, out in enumerate(outs):
        at = pl.ds(pl.multiple_of(((place + k) % depth) * part, 8), part)
        out[:, :LANES] = picked[at, :]
        lanes = iota((part, LANES), 1)
        out[:, LANES:] = jnp.where((base[0] == 0) & (lanes < top), block[at, :LANES], 0.0)


def gather_kernel(top, arrived, *refs):
    pieces, (shares, packed) = refs[:-2], refs[-2:]
    width = shares.shape[2]
    share = arrived[0, :, :width]
    for g in range(shares.shape[0]):
        shares[g] = share
    total = pieces[0][...]
    for piece in pieces[1:]:
        total = total + piece[...]
    square = arrived[0, :, width : width + LANES]
    begin = arrived[0, :, width + LANES :]
    third = LANES - top
    tail = iota(square.shape, 1) >= top
    for n, body in enumerate((total[:, :LANES], total[:, LANES:], square)):
        moved = pltpu.roll(begin, top - n * third, 1)
        packed[:, n * LANES : (n + 1) * LANES] = jnp.where(tail, moved, body)


def heads_kernel(top, place, *refs):
    pieces, (heads, square) = refs[:-2], refs[-2:]
    depth = len(pieces)
    part = pieces[0].shape[0]
    third = LANES - top
    lanes = iota((part, LANES), 1)
    total = pieces[0][...]
    for piece in pieces[1:]:
        total = total + piece[...]
    square[:, :LANES] = jnp.where(lanes < top, total[:, 2 * LANES :], 0.0)
    begin = jnp.zeros((part, LANES), F32)
    for n in range(3):
        moved = pltpu.roll(total[:, n * LANES : (n + 1) * LANES], LANES - top + n * third, 1)
        begin = jnp.where((lanes >= n * third) & (lanes < (n + 1) * third), moved, begin)
    square[:, LANES:] = begin
    keep = iota((part, 2 * LANES), 1) % LANES < top
    for k, piece in enumerate(pieces):
        owner = (place[0] + depth - k) % depth
        at = pl.ds(pl.multiple_of(owner * part, 8), part)
        heads[at, :] = jnp.where(keep, piece[:, : 2 * LANES], 0.0)


def spread(tile, j):
    return jnp.broadcast_to(tile[:, j : j + 1], (8, LANES))


def spread_row(tile, i):
    return jnp.broadcast_to(tile[i : i + 1, :], (8, LANES))


def reciprocal(x):
    r = pl.reciprocal(x, approx=True)
    r = r * (2.0 - x * r)
    return r * (2.0 - x * r)


def factor_kernel(core, mine, other, factor, lower_inv, upper_inv, starts):
    half = mine.shape[0]
    extent = 2 * half
    first = core[0] == 0
    m = mine[...]
    o = other[...]
    lo = jnp.where(first, m, o)
    hi = jnp.where(first, o, m)
    starts[:half, :] = lo[:, LANES:]
    starts[half:extent, :] = hi[:, LANES:]
    rest = jnp.zeros((LANES - extent, LANES), F32)
    starts[extent:, :] = rest
    tiles = [lo[8 * t : 8 * t + 8, :LANES] for t in range(half // 8)]
    tiles += [hi[8 * t : 8 * t + 8, :LANES] for t in range(half // 8)]
    square = jnp.concatenate(tiles + [rest], axis=0)
    lanes = iota((8, LANES), 1)
    subs = iota((8, LANES), 0)
    ahead = 2
    window = [[spread(t, q) for t in tiles] for q in range(ahead)]
    for j in range(extent):
        tj, sj = j // 8, j % 8
        here = lanes == j
        right = lanes > j
        cols = window.pop(0)
        if j + ahead < extent:
            window.append([spread(t, j + ahead) for t in tiles])
        row = spread_row(tiles[tj], sj)
        recip = reciprocal(spread_row(cols[tj], sj))
        scaled = jnp.where(here, recip, row * recip)
        right_part = jnp.where(right, scaled, 0.0)
        factor[j : j + 1, :] = right_part[:1]
        for q, nxt in enumerate(window):
            gain = spread_row(nxt[tj], sj) * recip
            moved = []
            for t, (n, col) in enumerate(zip(nxt, cols)):
                after = n - col * gain
                if t == tj:
                    after = jnp.where(subs == sj, -gain, after)
                moved.append(after)
            window[q] = moved
        new = []
        for t, (tile, col) in enumerate(zip(tiles, cols)):
            if t < tj:
                new.append(tile - col * right_part)
                continue
            below = jnp.where(here, 0.0, tile) - col * scaled
            if t == tj:
                above = tile - col * right_part
                at = jnp.where(right, -scaled, scaled)
                below = jnp.where(subs < sj, above, jnp.where(subs == sj, at, below))
            new.append(below)
        tiles = new
    for t, tile in enumerate(tiles):
        rows = subs + 8 * t
        at = pl.ds(8 * t, 8)
        lower_inv[at, :] = jnp.where(
            lanes > rows, jnp.where(lanes < extent, tile, 0.0), jnp.where(lanes == rows, 1.0, 0.0)
        )
        upper_inv[at, :] = jnp.where(lanes <= rows, tile, 0.0)
    factor[extent:, :] = rest
    lower_inv[extent:, :] = rest
    upper_inv[extent:, :] = rest
    upper = jnp.dot(square, lower_inv[...], precision=HI, preferred_element_type=F32)
    for t in range(extent // 8):
        at = pl.ds(8 * t, 8)
        rows = subs + 8 * t
        factor[at, :] = jnp.where(lanes > rows, factor[at, :], upper[8 * t : 8 * t + 8])


def split(x):
    head = x.astype(BF16)
    return head, (x - head.astype(F32)).astype(BF16)


def update_kernel(
    top, flags, heads, factor, lower_inv, upper_inv, starts, dest, block, mine, other, out,
    lhs_a, lhs_b, lhs_c, top_out,
):
    step = pl.program_id(0)
    half = mine.shape[1]
    width = block.shape[1]
    core, root, base = flags[0], flags[1], flags[2]

    @pl.when(step == 0)
    def _():
        tops = heads[:, :LANES]
        solved = jnp.dot(tops, lower_inv[...], precision=HI, preferred_element_type=F32)
        weight = jnp.dot(solved, upper_inv[...], precision=HI, preferred_element_type=F32)
        own_inv = jnp.where(core == 0, upper_inv[:half, :], upper_inv[half : 2 * half, :])
        own_fac = jnp.where(core == 0, factor[:half, :], factor[half : 2 * half, :])
        begin = heads[:, LANES:]
        is_root = root == 1
        weight = jnp.concatenate(
            [jnp.where(is_root, -own_inv, weight[:half]), weight[half:]], axis=0
        )
        begin = jnp.concatenate([jnp.where(is_root, 0.0, begin[:half]), begin[half:]], axis=0)
        top_out[...] = jnp.concatenate(
            [jnp.where(is_root, own_fac, solved[:half]), solved[half:]], axis=0
        )
        moved = begin - jnp.dot(weight, starts[...], precision=HI, preferred_element_type=F32)
        w_hi, w_lo = split(-weight)
        z_hi = moved.astype(BF16)
        left = moved - z_hi.astype(F32)
        z_mid, z_lo = split(left)
        lhs_a[:, :LANES] = w_hi
        lhs_a[:, LANES:] = z_hi
        lhs_b[:, :LANES] = w_lo
        lhs_b[:, LANES:] = z_mid
        lhs_c[:, :LANES] = w_hi
        lhs_c[:, LANES:] = z_lo

    groups = mine.shape[0]
    for g in range(groups):
        w = width // groups
        cols = slice(g * w, (g + 1) * w)
        m, o = mine[g], other[g]
        panel = jnp.concatenate([jnp.where(core == 0, m, o), jnp.where(core == 0, o, m)], axis=0)
        where_to = jnp.concatenate([dest[...]] * (w // LANES), axis=1)
        place = base + step * width + g * w + iota((LANES, w), 1)
        hot = jnp.where(where_to == place, 1.0, 0.0)
        keep = 1.0 - jnp.sum(hot, axis=0, keepdims=True)
        p_hi, p_lo = split(panel * keep)
        hot = hot.astype(BF16)
        fill = jnp.zeros((LANES - 2 * half, w), BF16)
        rhs_a = jnp.concatenate([p_hi, fill, hot], axis=0)
        rhs_c = jnp.concatenate([p_lo, fill, hot], axis=0)
        acc = jnp.dot(lhs_a[...], rhs_a, preferred_element_type=F32)
        acc += jnp.dot(lhs_b[...], rhs_a, preferred_element_type=F32)
        acc += jnp.dot(lhs_c[...], rhs_c, preferred_element_type=F32)
        keep_root = jnp.where(root == 1, 0.0, keep)
        out[:half, cols] = block[:half, cols] * keep_root + acc[:half]
        out[half:, cols] = block[half:, cols] * keep + acc[half:]

    @pl.when((step == 0) & (base == 0))
    def _():
        lanes = iota((block.shape[0], LANES), 1)
        out[:, :LANES] = jnp.where(lanes < top, top_out[...], out[:, :LANES])


def on_device(matrix, pivots):
    blocks, _, half, rows = matrix.shape
    cols = blocks * half
    top = 2 * half
    plane = ("y", "x")
    chips = lax.axis_size("y") * lax.axis_size("x")
    depth = lax.axis_size("prow")
    width = rows // chips
    holdings = matrix.reshape(cols, rows)
    core = lax.axis_index("core").astype(jnp.int32)
    base = (lax.axis_index("prow") * rows).astype(jnp.int32)
    root = ((lax.axis_index("y") == 0) & (lax.axis_index("x") == 0)).astype(jnp.int32)
    base1 = base.reshape(1)
    swap = [(0, 1), (1, 0)]

    def around(step):
        return [(z, (z + step) % depth) for z in range(depth)]

    def call(kernel, name, us, out_shape, in_specs, out_specs, *args, **more):
        return pl.pallas_call(
            lambda *refs: kernel(top, *refs),
            out_shape=out_shape,
            in_specs=in_specs,
            out_specs=out_specs,
            compiler_params=params(),
            cost_estimate=cost(us),
            name=name,
            **more,
        )(*args)

    blocks16, wanted, dest = call(
        start_kernel,
        "start",
        5,
        (
            jax.ShapeDtypeStruct((chips, half, width + 2 * LANES), F32),
            jax.ShapeDtypeStruct((top,), jnp.int32),
            jax.ShapeDtypeStruct((LANES, LANES), jnp.int32),
        ),
        [smem_spec(), smem_spec(), pl.BlockSpec((half, rows), lambda i: (0, 0))],
        (vmem_spec(), smem_spec(), vmem_spec()),
        pivots,
        base1,
        holdings,
        grid=(1,),
        scratch_shapes=[
            pltpu.SMEM((rows * depth,), jnp.int32),
            pltpu.SMEM((top + 8,), jnp.int32),
            pltpu.VMEM((half, LANES), F32),
        ],
    )
    arrived = lax.all_to_all(blocks16, plane, 0, 0)
    piece = jax.ShapeDtypeStruct((cols // depth, 2 * LANES), F32)
    offered = call(
        own_kernel,
        "own",
        5,
        (piece,) * depth,
        [smem_spec(), smem_spec(), vmem_spec()],
        (vmem_spec(),) * depth,
        base1,
        wanted,
        holdings,
        scratch_shapes=[pltpu.VMEM((cols, LANES), F32)],
    )
    pieces = [offered[0]]
    pieces += [lax.ppermute(offered[k], "prow", around(k)) for k in range(1, depth)]
    shares, packed = call(
        gather_kernel,
        "gather",
        2,
        (
            jax.ShapeDtypeStruct((chips, half, width), F32),
            jax.ShapeDtypeStruct((half, 3 * LANES), F32),
        ),
        [pl.BlockSpec((1, half, width + 2 * LANES), lambda i: (0, 0, 0))]
        + [pl.BlockSpec(piece.shape, lambda i: (0, 0))] * depth,
        (vmem_spec(), vmem_spec()),
        arrived,
        *pieces,
        grid=(1,),
    )
    mine = lax.all_to_all(shares, plane, 0, 0)
    slices = [packed] + [lax.ppermute(packed, "prow", around(k)) for k in range(1, depth)]
    heads, square = call(
        heads_kernel,
        "heads",
        1,
        (
            jax.ShapeDtypeStruct((cols, 2 * LANES), F32),
            jax.ShapeDtypeStruct((half, 2 * LANES), F32),
        ),
        [smem_spec()] + [vmem_spec()] * depth,
        (vmem_spec(), vmem_spec()),
        base1 // rows,
        *slices,
    )
    square_other = lax.ppermute(square, "core", swap)
    mine, square_other = lax.optimization_barrier((mine, square_other))
    other = lax.ppermute(mine, "core", swap)
    small = jax.ShapeDtypeStruct((LANES, LANES), F32)
    factor, lower_inv, upper_inv, starts = pl.pallas_call(
        factor_kernel,
        out_shape=(small,) * 4,
        in_specs=[smem_spec(), vmem_spec(), vmem_spec()],
        out_specs=(vmem_spec(),) * 4,
        compiler_params=params(),
        cost_estimate=cost(9),
        name="factor",
    )(core.reshape(1), square, square_other)
    flags = jnp.stack([core, root, base])
    per_step = 4
    span = per_step * width
    whole = pl.BlockSpec((LANES, LANES), lambda i: (0, 0))
    parts = pl.BlockSpec((per_step, half, width), lambda i: (i, 0, 0))
    result = pl.pallas_call(
        lambda *refs: update_kernel(top, *refs),
        grid=(rows // span,),
        out_shape=jax.ShapeDtypeStruct((cols, rows), F32),
        in_specs=[
            smem_spec(),
            pl.BlockSpec((cols, 2 * LANES), lambda i: (0, 0)),
            whole,
            whole,
            whole,
            whole,
            whole,
            pl.BlockSpec((cols, span), lambda i: (0, i)),
            parts,
            parts,
        ],
        out_specs=pl.BlockSpec((cols, span), lambda i: (0, i)),
        scratch_shapes=[
            pltpu.VMEM((cols, 2 * LANES), BF16),
            pltpu.VMEM((cols, 2 * LANES), BF16),
            pltpu.VMEM((cols, 2 * LANES), BF16),
            pltpu.VMEM((cols, LANES), F32),
        ],
        compiler_params=params(),
        cost_estimate=cost(8),
        name="update",
    )(flags, heads, factor, lower_inv, upper_inv, starts, dest, holdings, mine, other)
    return result.reshape(matrix.shape)


def solution(mesh):
    fine = Mesh(mesh.devices.reshape(4, 4, 2, 8), ("y", "x", "core", "prow"))
    spec = P(None, ("y", "x", "core"), None, "prow")
    return jax.shard_map(
        on_device, mesh=fine, in_specs=(spec, P()), out_specs=spec, check_vma=False
    )
```

time: 1970 us -> 88.2 us (0.04)
  other arithmetic: 679 us -> 0.08 us
  local copies, waits for them, and re-layouts: 578 us -> 0.65 us
  blocking collectives: 248 us -> 0 us
  loops' own time: 214 us -> 0 us
  waiting for transfers between devices: 212 us -> 16.1 us
  starting transfers between devices: 0.27 us -> 43.1 us
  Pallas kernels: 0 us -> 27.2 us
  matrix products: 19.7 us -> 0 us
    another operation x389 -> x1, other arithmetic: 396 us -> 0.08 us  [on_device(): flags = jnp.stack([core, root, base])]
    dynamic_slice x480 -> x0, local copies, waits for them, and re-layouts: 304 us -> none  [the longest x96 126 us: compose_advance(): target = swap_targets[counter]]
    psum x2 -> x0, blocking collectives: 248 us -> none  [broadcast(): return lax.psum(jnp.where(mine, shard, jnp.zeros_like(shard)), axis)]
    another operation x9 -> x0, loops' own time: 214 us -> none  [the longest x1 200 us: compose(): return lax.fori_loop(0, swap_targets.shape[0], compose_advance, ordering)]
    psum x3 -> x0, waiting for transfers between devices: 212 us -> none  [broadcast(): return lax.psum(jnp.where(mine, shard, jnp.zeros_like(shard)), axis)]
    scatter x296 -> x0, local copies, waits for them, and re-layouts: 184 us -> none  [the longest x1 120 us: on_device(): inverse_order = jnp.zeros((total_rows,), jnp.int32).at[ordering].set(jnp....]
    scatter x196 -> x0, other arithmetic: 171 us -> none  [the longest x192 169 us: compose_advance(): return current.at[counter].set(at_target).at[target].set(at_counter)]
    mul x480 -> x0, other arithmetic: 64.6 us -> none  [the longest x192 61.1 us: eliminate_advance(): jnp.where(beneath, column, 0.0)[:, None]]
  transfers between devices with their start and end apart: 3 -> 18, of which waited for: 2 -> 7; matrix products, arithmetic and copies ran while one was open for 7% -> 0% of each run, Pallas kernels for 0% -> 14%
where the time goes in v1:
time: 88.2 us; the launch traced here: 87.2 us
  starting transfers between devices  43.1 us (49%)
  Pallas kernels  27.2 us (31%)
  waiting for transfers between devices  16.1 us (18%)
    ppermute x7, starting transfers between devices, on_device(): lax.ppermute(offered[k], 'prow', around(k))  15.6 us
    pallas_call x4, Pallas kernels, call(): pl.pallas_call(lambda *refs: kernel(top, *refs), out_shape=out_shape, in_...  12.9 us
    ppermute x7, starting transfers between devices, on_device(): lax.ppermute(packed, 'prow', around(k))  10.8 us
    ppermute x7, waiting for transfers between devices, on_device(): lax.ppermute(packed, 'prow', around(k))  10.2 us
    pallas_call x1, Pallas kernels, on_device(): pl.pallas_call(lambda *refs: update_kernel(top, *refs), grid=(rows // spa...  8.69 us
    all_to_all x1, starting transfers between devices, on_device(): arrived = lax.all_to_all(blocks16, plane, 0, 0)  7.6 us
    all_to_all x1, starting transfers between devices, on_device(): mine = lax.all_to_all(shares, plane, 0, 0)  5.62 us
    pallas_call x1, Pallas kernels, on_device(): pl.pallas_call(factor_kernel, out_shape=(small,) * 4, in_specs=[smem_spec...  5.55 us
  transfers between devices with their start and end apart: 18, of which 7 were waited for; matrix products, arithmetic and copies ran while one was open for 0% of the time, Pallas kernels for 14%

profile of v1, /device:TPU:1, one launch (start us, length us, event | category | flops | bytes accessed | tf_op | source)
XLA Modules:
  0.0 87.2 jit_solution(11075183183942081856)
XLA Ops:
  0.0 0.7 copy-done
  0.7 5.4 %start.1 = (f32[16,48,512]{2,1,0:T(8,128)}, s32[96]{0:T(128)S(1)}, s32[128,128]{1,0:T(8,128)S(1)}) custom-call(s32[96]{0:T(128)S(1)} %copy-done, s32[1]{0:T(128)} %bitcast.2.refs_1_.refs_0_, f32[384,4096]{1,0:T(8,128)} %bitcast.7), custom_call_target="tpu_custom_call" | custom-call | bytes 17500000 | tf_op jit(solution)/shard_map/start/pallas_call | solution.py:322
  6.1 7.6 %all-to-all-start = ((f32[16,48,512]{2,1,0:T(8,128)}), f32[16,48,512]{2,1,0:T(8,128)S(1)}, u32[]{:S(2)}, u32[]{:S(2)}) async-start(f32[16,48,512]{2,1,0:T(8,128)} %get-tuple-element.26), calls=%async_computation | async-start | bytes 3145728 | tf_op jit(solution)/shard_map/all_to_all | solution.py:354
  13.7 6.4 %own.1 = (f32[48,256]{1,0:T(8,128)S(1)}, f32[48,256]{1,0:T(8,128)S(1)}, f32[48,256]{1,0:T(8,128)S(1)}, f32[48,256]{1,0:T(8,128)S(1)}, f32[48,256]{1,0:T(8,128)S(...) custom-call(s32[1]{0:T(128)} %bitcast.2.refs_1_.refs_0_, ...), custom_call_target="tpu_custom_call" | custom-call | bytes 17500000 | tf_op jit(solution)/shard_map/own/pallas_call | solution.py:322
  20.1 0.1 collective-permute-start
  20.2 3.6 %collective-permute-start.1 = (f32[48,256]{1,0:T(8,128)S(1)}, f32[48,256]{1,0:T(8,128)S(1)}, u32[]{:S(2)}, u32[]{:S(2)}) collective-permute-start(f32[48,256]{1,0:T(8,128)S(1)} %get-tuple-element.30), channel_id=1, source_target_pairs={{0,2},{1,3},{2,4},{3,5},{4,6},{5,7},{6,0},{7,1},{8,10},{9,11},{10,... | collective-permute-start | bytes 147464 | tf_op jit(solution)/shard_map/ppermute | solution.py:369
  23.8 3.6 %collective-permute-start.2 = (f32[48,256]{1,0:T(8,128)S(1)}, f32[48,256]{1,0:T(8,128)S(1)}, u32[]{:S(2)}, u32[]{:S(2)}) collective-permute-start(f32[48,256]{1,0:T(8,128)S(1)} %get-tuple-element.31), channel_id=1, source_target_pairs={{0,3},{1,4},{2,5},{3,6},{4,7},{5,0},{6,1},{7,2},{8,11},{9,12},{10,... | collective-permute-start | bytes 147464 | tf_op jit(solution)/shard_map/ppermute | solution.py:369
  27.5 0.5 collective-permute-start.3
  27.9 4.5 %collective-permute-start.4 = (f32[48,256]{1,0:T(8,128)S(1)}, f32[48,256]{1,0:T(8,128)S(1)}, u32[]{:S(2)}, u32[]{:S(2)}) collective-permute-start(f32[48,256]{1,0:T(8,128)S(1)} %get-tuple-element.33), channel_id=1, source_target_pairs={{0,5},{1,6},{2,7},{3,0},{4,1},{5,2},{6,3},{7,4},{8,13},{9,14},{10,... | collective-permute-start | bytes 147464 | tf_op jit(solution)/shard_map/ppermute | solution.py:369
  32.4 3.0 %collective-permute-start.5 = (f32[48,256]{1,0:T(8,128)S(1)}, f32[48,256]{1,0:T(8,128)S(1)}, u32[]{:S(2)}, u32[]{:S(2)}) collective-permute-start(f32[48,256]{1,0:T(8,128)S(1)} %get-tuple-element.34), channel_id=1, source_target_pairs={{0,6},{1,7},{2,0},{3,1},{4,2},{5,3},{6,4},{7,5},{8,14},{9,15},{10,... | collective-permute-start | bytes 147464 | tf_op jit(solution)/shard_map/ppermute | solution.py:369
  35.4 0.3 collective-permute-start.6
  35.7 0.6 collective-permute-done.4.refs_6_
  36.4 2.3 %collective-permute-done.5.refs_7_ = f32[48,256]{1,0:T(8,128)S(1)} collective-permute-done((f32[48,256]{1,0:T(8,128)S(1)}, f32[48,256]{1,0:T(8,128)S(1)}, u32[]{:S(2)}, u32[]{:S(2)}) %collective-permute-start.5) | collective-permute-done | bytes 49184 | tf_op jit(solution)/shard_map/ppermute | solution.py:369
  38.7 2.1 %collective-permute-done.6.refs_8_ = f32[48,256]{1,0:T(8,128)S(1)} collective-permute-done((f32[48,256]{1,0:T(8,128)S(1)}, f32[48,256]{1,0:T(8,128)S(1)}, u32[]{:S(2)}, u32[]{:S(2)}) %collective-permute-start.6) | collective-permute-done | bytes 49184 | tf_op jit(solution)/shard_map/ppermute | solution.py:369
  40.8 1.0 %gather.1 = (f32[16,48,256]{2,1,0:T(8,128)}, f32[48,384]{1,0:T(8,128)S(1)}) custom-call(f32[16,48,512]{2,1,0:T(8,128)S(1)} %all-to-all-done.refs_0_, f32[48,256]{1,0:T(8,128)S(1)} %get-tuple-element.28.refs_1_, f32[48,256]{1,0:T(8,128)S(1)} %collective-permute-done.refs_2_, f32[48,256]{1,0:T(8,128)S(1)} %collective-permute-done.1.refs_3_, ...), custom_call_target="tpu_custom_call" | custom-call | bytes 7000000 | tf_op jit(solution)/shard_map/gather/pallas_call | solution.py:322
  41.8 5.6 %all-to-all-start.1 = ((f32[16,48,256]{2,1,0:T(8,128)}), f32[16,48,256]{2,1,0:T(8,128)S(1)}, u32[]{:S(2)}, u32[]{:S(2)}) async-start(f32[16,48,256]{2,1,0:T(8,128)} %get-tuple-element.39), calls=%async_computation.1 | async-start | bytes 1572864 | tf_op jit(solution)/shard_map/all_to_all | solution.py:385
  47.4 2.8 %collective-permute-start.13 = (f32[48,384]{1,0:T(8,128)S(1)}, f32[48,384]{1,0:T(8,128)S(1)}, u32[]{:S(2)}, u32[]{:S(2)}) collective-permute-start(f32[48,384]{1,0:T(8,128)S(1)} %get-tuple-element.36.refs_1_), channel_id=1, source_target_pairs={{0,7},{1,0},{2,1},{3,2},{4,3},{5,4},{6,5},{7,6},{8,15},{9,8},{10,9... | collective-permute-start | bytes 221192 | tf_op jit(solution)/shard_map/ppermute | solution.py:386
  50.2 1.1 %collective-permute-start.11 = (f32[48,384]{1,0:T(8,128)S(1)}, f32[48,384]{1,0:T(8,128)S(1)}, u32[]{:S(2)}, u32[]{:S(2)}) collective-permute-start(f32[48,384]{1,0:T(8,128)S(1)} %get-tuple-element.36.refs_1_), channel_id=1, source_target_pairs={{0,5},{1,6},{2,7},{3,0},{4,1},{5,2},{6,3},{7,4},{8,13},{9,14},{10,... | collective-permute-start | bytes 221192 | tf_op jit(solution)/shard_map/ppermute | solution.py:386
  51.3 4.5 %collective-permute-start.10 = (f32[48,384]{1,0:T(8,128)S(1)}, f32[48,384]{1,0:T(8,128)S(1)}, u32[]{:S(2)}, u32[]{:S(2)}) collective-permute-start(f32[48,384]{1,0:T(8,128)S(1)} %get-tuple-element.36.refs_1_), channel_id=1, source_target_pairs={{0,4},{1,5},{2,6},{3,7},{4,0},{5,1},{6,2},{7,3},{8,12},{9,13},{10,... | collective-permute-start | bytes 221192 | tf_op jit(solution)/shard_map/ppermute | solution.py:386
  55.8 0.9 %collective-permute-start.9 = (f32[48,384]{1,0:T(8,128)S(1)}, f32[48,384]{1,0:T(8,128)S(1)}, u32[]{:S(2)}, u32[]{:S(2)}) collective-permute-start(f32[48,384]{1,0:T(8,128)S(1)} %get-tuple-element.36.refs_1_), channel_id=1, source_target_pairs={{0,3},{1,4},{2,5},{3,6},{4,7},{5,0},{6,1},{7,2},{8,11},{9,12},{10,... | collective-permute-start | bytes 221192 | tf_op jit(solution)/shard_map/ppermute | solution.py:386
  56.7 1.0 %collective-permute-start.8 = (f32[48,384]{1,0:T(8,128)S(1)}, f32[48,384]{1,0:T(8,128)S(1)}, u32[]{:S(2)}, u32[]{:S(2)}) collective-permute-start(f32[48,384]{1,0:T(8,128)S(1)} %get-tuple-element.36.refs_1_), channel_id=1, source_target_pairs={{0,2},{1,3},{2,4},{3,5},{4,6},{5,7},{6,0},{7,1},{8,10},{9,11},{10,... | collective-permute-start | bytes 221192 | tf_op jit(solution)/shard_map/ppermute | solution.py:386
  57.7 0.5 collective-permute-start.7
  58.3 0.3 collective-permute-done.10.refs_5_
  58.6 5.4 %collective-permute-done.9.refs_4_ = f32[48,384]{1,0:T(8,128)S(1)} collective-permute-done((f32[48,384]{1,0:T(8,128)S(1)}, f32[48,384]{1,0:T(8,128)S(1)}, u32[]{:S(2)}, u32[]{:S(2)}) %collective-permute-start.9) | collective-permute-done | bytes 73760 | tf_op jit(solution)/shard_map/ppermute | solution.py:386
  64.0 4.4 %collective-permute-done.8.refs_3_ = f32[48,384]{1,0:T(8,128)S(1)} collective-permute-done((f32[48,384]{1,0:T(8,128)S(1)}, f32[48,384]{1,0:T(8,128)S(1)}, u32[]{:S(2)}, u32[]{:S(2)}) %collective-permute-start.8) | collective-permute-done | bytes 73760 | tf_op jit(solution)/shard_map/ppermute | solution.py:386
  68.4 0.1 heads.1
  68.5 3.1 %collective-permute-start.14 = (f32[48,256]{1,0:T(8,128)S(1)}, f32[48,256]{1,0:T(8,128)S(1)}, u32[]{:S(2)}, u32[]{:S(2)}) collective-permute-start(f32[48,256]{1,0:T(8,128)S(1)} %get-tuple-element.38.mine), channel_id=1, source_target_pairs={{0,8},{8,0},{1,9},{9,1},{2,10},{10,2},{3,11},{11,3},{4,12},{12,4},... | collective-permute-start | bytes 147464 | tf_op jit(solution)/shard_map/ppermute | solution.py:400
  71.6 0.9 %collective-permute-done.14.other = f32[48,256]{1,0:T(8,128)S(1)} collective-permute-done((f32[48,256]{1,0:T(8,128)S(1)}, f32[48,256]{1,0:T(8,128)S(1)}, u32[]{:S(2)}, u32[]{:S(2)}) %collective-permute-start.14) | collective-permute-done | bytes 49184 | tf_op jit(solution)/shard_map/ppermute | solution.py:400
  72.5 0.4 collective-permute-start.15
  72.8 0.1 pad_add_fusion.refs_0_
  72.9 5.5 %factor.1 = (f32[128,128]{1,0:T(8,128)S(1)}, f32[128,128]{1,0:T(8,128)S(1)}, f32[128,128]{1,0:T(8,128)S(1)}, f32[128,128]{1,0:T(8,128)S(1)}) custom-call(s32[1]{0:T(128)} %bitcast.core, f32[48,256]{1,0:T(8,128)S(1)} %get-tuple-element.38.mine, f32[48,256]{1,0:T(8,128)S(1)} %collective-permute-done.14.other), custom_call_target="tpu_custom_call" | custom-call | bytes 31500000 | tf_op jit(solution)/shard_map/factor/pallas_call | solution.py:404
  78.5 8.7 %update.1 = f32[384,4096]{1,0:T(8,128)} custom-call(s32[3]{0:T(128)S(1)} %pad_add_fusion.refs_0_, f32[384,256]{1,0:T(8,128)S(1)} %get-tuple-element.37.refs_1_, f32[128,128]{1,0:T(8,128)S(1)} %get-tuple-element.41.refs_2_, f32[128,128]{1,0:T(8,128)S(1)} %get-tuple-element.42.refs_3_, f32[128,128]{1,0:T(8,128)S(1)} %get-tuple-element.43.refs_4_, ...), custom_call_target="tpu_custom_call" | custom-call | bytes 28000000 | tf_op jit(solution)/shard_map/update/pallas_call | solution.py:418
  (13 shorter events, 0.0 us)
Async XLA Ops:
  0.0 0.7 copy-start
  6.1 34.8 %all-to-all-start = ((f32[16,48,512]{2,1,0:T(8,128)}), f32[16,48,512]{2,1,0:T(8,128)S(1)}, u32[]{:S(2)}, u32[]{:S(2)}) async-start(f32[16,48,512]{2,1,0:T(8,128)} %get-tuple-element.26), calls=%async_computation | async-start | bytes 3145728 | tf_op jit(solution)/shard_map/all_to_all | solution.py:354
  20.1 12.3 %collective-permute-start = (f32[48,256]{1,0:T(8,128)S(1)}, f32[48,256]{1,0:T(8,128)S(1)}, u32[]{:S(2)}, u32[]{:S(2)}) collective-permute-start(f32[48,256]{1,0:T(8,128)S(1)} %get-tuple-element.29), channel_id=1, source_target_pairs={{0,1},{1,2},{2,3},{3,4},{4,5},{5,6},{6,7},{7,0},{8,9},{9,10},{10,1... | collective-permute-start | bytes 147464 | tf_op jit(solution)/shard_map/ppermute | solution.py:369
  20.2 15.2 %collective-permute-start.1 = (f32[48,256]{1,0:T(8,128)S(1)}, f32[48,256]{1,0:T(8,128)S(1)}, u32[]{:S(2)}, u32[]{:S(2)}) collective-permute-start(f32[48,256]{1,0:T(8,128)S(1)} %get-tuple-element.30), channel_id=1, source_target_pairs={{0,2},{1,3},{2,4},{3,5},{4,6},{5,7},{6,0},{7,1},{8,10},{9,11},{10,... | collective-permute-start | bytes 147464 | tf_op jit(solution)/shard_map/ppermute | solution.py:369
  23.8 11.9 %collective-permute-start.2 = (f32[48,256]{1,0:T(8,128)S(1)}, f32[48,256]{1,0:T(8,128)S(1)}, u32[]{:S(2)}, u32[]{:S(2)}) collective-permute-start(f32[48,256]{1,0:T(8,128)S(1)} %get-tuple-element.31), channel_id=1, source_target_pairs={{0,3},{1,4},{2,5},{3,6},{4,7},{5,0},{6,1},{7,2},{8,11},{9,12},{10,... | collective-permute-start | bytes 147464 | tf_op jit(solution)/shard_map/ppermute | solution.py:369
  27.5 8.3 %collective-permute-start.3 = (f32[48,256]{1,0:T(8,128)S(1)}, f32[48,256]{1,0:T(8,128)S(1)}, u32[]{:S(2)}, u32[]{:S(2)}) collective-permute-start(f32[48,256]{1,0:T(8,128)S(1)} %get-tuple-element.32), channel_id=1, source_target_pairs={{0,4},{1,5},{2,6},{3,7},{4,0},{5,1},{6,2},{7,3},{8,12},{9,13},{10,... | collective-permute-start | bytes 147464 | tf_op jit(solution)/shard_map/ppermute | solution.py:369
  27.9 8.5 %collective-permute-start.4 = (f32[48,256]{1,0:T(8,128)S(1)}, f32[48,256]{1,0:T(8,128)S(1)}, u32[]{:S(2)}, u32[]{:S(2)}) collective-permute-start(f32[48,256]{1,0:T(8,128)S(1)} %get-tuple-element.33), channel_id=1, source_target_pairs={{0,5},{1,6},{2,7},{3,0},{4,1},{5,2},{6,3},{7,4},{8,13},{9,14},{10,... | collective-permute-start | bytes 147464 | tf_op jit(solution)/shard_map/ppermute | solution.py:369
  32.4 6.3 %collective-permute-start.5 = (f32[48,256]{1,0:T(8,128)S(1)}, f32[48,256]{1,0:T(8,128)S(1)}, u32[]{:S(2)}, u32[]{:S(2)}) collective-permute-start(f32[48,256]{1,0:T(8,128)S(1)} %get-tuple-element.34), channel_id=1, source_target_pairs={{0,6},{1,7},{2,0},{3,1},{4,2},{5,3},{6,4},{7,5},{8,14},{9,15},{10,... | collective-permute-start | bytes 147464 | tf_op jit(solution)/shard_map/ppermute | solution.py:369
  35.4 5.4 %collective-permute-start.6 = (f32[48,256]{1,0:T(8,128)S(1)}, f32[48,256]{1,0:T(8,128)S(1)}, u32[]{:S(2)}, u32[]{:S(2)}) collective-permute-start(f32[48,256]{1,0:T(8,128)S(1)} %get-tuple-element.35), channel_id=1, source_target_pairs={{0,7},{1,0},{2,1},{3,2},{4,3},{5,4},{6,5},{7,6},{8,15},{9,8},{10,9... | collective-permute-start | bytes 147464 | tf_op jit(solution)/shard_map/ppermute | solution.py:369
  41.8 30.7 %all-to-all-start.1 = ((f32[16,48,256]{2,1,0:T(8,128)}), f32[16,48,256]{2,1,0:T(8,128)S(1)}, u32[]{:S(2)}, u32[]{:S(2)}) async-start(f32[16,48,256]{2,1,0:T(8,128)} %get-tuple-element.39), calls=%async_computation.1 | async-start | bytes 1572864 | tf_op jit(solution)/shard_map/all_to_all | solution.py:385
  47.4 9.3 %collective-permute-start.13 = (f32[48,384]{1,0:T(8,128)S(1)}, f32[48,384]{1,0:T(8,128)S(1)}, u32[]{:S(2)}, u32[]{:S(2)}) collective-permute-start(f32[48,384]{1,0:T(8,128)S(1)} %get-tuple-element.36.refs_1_), channel_id=1, source_target_pairs={{0,7},{1,0},{2,1},{3,2},{4,3},{5,4},{6,5},{7,6},{8,15},{9,8},{10,9... | collective-permute-start | bytes 221192 | tf_op jit(solution)/shard_map/ppermute | solution.py:386
  50.2 7.5 %collective-permute-start.12 = (f32[48,384]{1,0:T(8,128)S(1)}, f32[48,384]{1,0:T(8,128)S(1)}, u32[]{:S(2)}, u32[]{:S(2)}) collective-permute-start(f32[48,384]{1,0:T(8,128)S(1)} %get-tuple-element.36.refs_1_), channel_id=1, source_target_pairs={{0,6},{1,7},{2,0},{3,1},{4,2},{5,3},{6,4},{7,5},{8,14},{9,15},{10,... | collective-permute-start | bytes 221192 | tf_op jit(solution)/shard_map/ppermute | solution.py:386
  50.2 8.0 %collective-permute-start.11 = (f32[48,384]{1,0:T(8,128)S(1)}, f32[48,384]{1,0:T(8,128)S(1)}, u32[]{:S(2)}, u32[]{:S(2)}) collective-permute-start(f32[48,384]{1,0:T(8,128)S(1)} %get-tuple-element.36.refs_1_), channel_id=1, source_target_pairs={{0,5},{1,6},{2,7},{3,0},{4,1},{5,2},{6,3},{7,4},{8,13},{9,14},{10,... | collective-permute-start | bytes 221192 | tf_op jit(solution)/shard_map/ppermute | solution.py:386
  51.3 7.3 %collective-permute-start.10 = (f32[48,384]{1,0:T(8,128)S(1)}, f32[48,384]{1,0:T(8,128)S(1)}, u32[]{:S(2)}, u32[]{:S(2)}) collective-permute-start(f32[48,384]{1,0:T(8,128)S(1)} %get-tuple-element.36.refs_1_), channel_id=1, source_target_pairs={{0,4},{1,5},{2,6},{3,7},{4,0},{5,1},{6,2},{7,3},{8,12},{9,13},{10,... | collective-permute-start | bytes 221192 | tf_op jit(solution)/shard_map/ppermute | solution.py:386
  55.8 8.3 %collective-permute-start.9 = (f32[48,384]{1,0:T(8,128)S(1)}, f32[48,384]{1,0:T(8,128)S(1)}, u32[]{:S(2)}, u32[]{:S(2)}) collective-permute-start(f32[48,384]{1,0:T(8,128)S(1)} %get-tuple-element.36.refs_1_), channel_id=1, source_target_pairs={{0,3},{1,4},{2,5},{3,6},{4,7},{5,0},{6,1},{7,2},{8,11},{9,12},{10,... | collective-permute-start | bytes 221192 | tf_op jit(solution)/shard_map/ppermute | solution.py:386
  56.7 11.7 %collective-permute-start.8 = (f32[48,384]{1,0:T(8,128)S(1)}, f32[48,384]{1,0:T(8,128)S(1)}, u32[]{:S(2)}, u32[]{:S(2)}) collective-permute-start(f32[48,384]{1,0:T(8,128)S(1)} %get-tuple-element.36.refs_1_), channel_id=1, source_target_pairs={{0,2},{1,3},{2,4},{3,5},{4,6},{5,7},{6,0},{7,1},{8,10},{9,11},{10,... | collective-permute-start | bytes 221192 | tf_op jit(solution)/shard_map/ppermute | solution.py:386
  57.7 10.7 %collective-permute-start.7 = (f32[48,384]{1,0:T(8,128)S(1)}, f32[48,384]{1,0:T(8,128)S(1)}, u32[]{:S(2)}, u32[]{:S(2)}) collective-permute-start(f32[48,384]{1,0:T(8,128)S(1)} %get-tuple-element.36.refs_1_), channel_id=1, source_target_pairs={{0,1},{1,2},{2,3},{3,4},{4,5},{5,6},{6,7},{7,0},{8,9},{9,10},{10,1... | collective-permute-start | bytes 221192 | tf_op jit(solution)/shard_map/ppermute | solution.py:386
  68.5 3.9 %collective-permute-start.14 = (f32[48,256]{1,0:T(8,128)S(1)}, f32[48,256]{1,0:T(8,128)S(1)}, u32[]{:S(2)}, u32[]{:S(2)}) collective-permute-start(f32[48,256]{1,0:T(8,128)S(1)} %get-tuple-element.38.mine), channel_id=1, source_target_pairs={{0,8},{8,0},{1,9},{9,1},{2,10},{10,2},{3,11},{11,3},{4,12},{12,4},... | collective-permute-start | bytes 147464 | tf_op jit(solution)/shard_map/ppermute | solution.py:400
  72.5 6.0 %collective-permute-start.15 = (f32[16,48,256]{2,1,0:T(8,128)S(1)}, f32[16,48,256]{2,1,0:T(8,128)S(1)}, u32[]{:S(2)}, u32[]{:S(2)}) collective-permute-start(f32[16,48,256]{2,1,0:T(8,128)S(1)} %all-to-all-done.1.refs_8_), channel_id=1, source_target_pairs={{0,8},{8,0},{1,9},{9,1},{2,10},{10,2},{3,11},{11,3},{4,12},{12,4},... | collective-permute-start | bytes 2359304 | tf_op jit(solution)/shard_map/ppermute | solution.py:402

commit v2 on v1

--- a/solution.py
+++ b/solution.py
@@ -32,29 +32,30 @@
     return pl.CostEstimate(flops=0, bytes_accessed=int(us * 3.5e6), transcendentals=0)
 
 
-def pick_rows(wanted, base, rows, block, out, top):
+def pick_rows(wanted, owned, base, block, out):
     lanes = iota((block.shape[0], LANES), 1)
 
-    def step(i, carry):
+    def step(n, carry):
+        i = owned[n]
         local = wanted[i] - base
 
-        @pl.when((local >= 0) & (local < rows))
+        @pl.when((local >= 0) & (local < block.shape[1]))
         def _():
             start = pl.multiple_of((local // LANES) * LANES, LANES)
             shift = (i + LANES - local % LANES) % LANES
             moved = pltpu.roll(block[:, pl.ds(start, LANES)], shift, 1)
-            out[...] = jnp.where(lanes == i, moved, out[...])
+            out[:, :LANES] = jnp.where(lanes == i, moved, out[:, :LANES])
 
         return carry
 
-    out[...] = jnp.zeros(out.shape, F32)
-    lax.fori_loop(0, top, step, 0)
-
-
-def start_kernel(top, pivots, base, panel, blocks, wanted, dest, current, goes, picked):
+    lax.fori_loop(0, owned[owned.shape[0] - 8], step, 0)
+
+
+def start_kernel(top, pivots, base, panel, *refs):
+    sends, (wanted, owned, dest, current, goes, picked) = refs[:-6], refs[-6:]
     rows = panel.shape[1]
-    groups = blocks.shape[0]
-    width = rows // groups
+    span = len(sends)
+    width = sends[0].shape[2]
 
     def fill(j, carry):
         current[pivots[j]] = pivots[j]
@@ -73,7 +74,9 @@
         current[t] = a
         goes[jnp.minimum(b, top)] = -1
         goes[a] = jnp.where(t >= top, t, -1)
-        return carry
+        owned[carry] = j
+        local = b - base[0]
+        return carry + ((local >= 0) & (local < rows)).astype(jnp.int32)
 
     def emit(j, carry):
         dest[pl.ds(j, 1), :] = jnp.full((1, LANES), goes[j], jnp.int32)
@@ -81,59 +84,90 @@
 
     lax.fori_loop(0, top, fill, 0, unroll=8)
     lax.fori_loop(0, top, fill_top, 0, unroll=8)
-    lax.fori_loop(0, top, swap, 0, unroll=8)
+    owned[top] = lax.fori_loop(0, top, swap, 0, unroll=8)
     dest[...] = jnp.full(dest.shape, -1, jnp.int32)
     lax.fori_loop(0, top, emit, 0, unroll=8)
-    pick_rows(wanted, base[0], rows, panel, picked, top)
+    picked[...] = jnp.zeros(picked.shape, F32)
+    pick_rows(wanted, owned, base[0], panel, picked)
     lanes = iota(picked.shape, 1)
     heads = jnp.where((base[0] == 0) & (lanes < top), panel[:, :LANES], 0.0)
-    for g in range(groups):
-        blocks[g, :, :width] = panel[:, g * width : (g + 1) * width]
-        blocks[g, :, width : width + LANES] = picked[...]
-        blocks[g, :, width + LANES :] = heads
-
-
-def own_kernel(top, base, wanted, block, *refs):
-    outs, picked = refs[:-1], refs[-1]
-    depth = len(outs)
-    rows = block.shape[1]
-    part = block.shape[0] // depth
-    pick_rows(wanted, base[0], rows, block, picked, top)
-    place = base[0] // rows
-    for k, out in enumerate(outs):
-        at = pl.ds(pl.multiple_of(((place + k) % depth) * part, 8), part)
-        out[:, :LANES] = picked[at, :]
-        lanes = iota((part, LANES), 1)
-        out[:, LANES:] = jnp.where((base[0] == 0) & (lanes < top), block[at, :LANES], 0.0)
-
-
-def gather_kernel(top, arrived, *refs):
-    pieces, (shares, packed) = refs[:-2], refs[-2:]
-    width = shares.shape[2]
-    share = arrived[0, :, :width]
-    for g in range(shares.shape[0]):
-        shares[g] = share
-    total = pieces[0][...]
-    for piece in pieces[1:]:
-        total = total + piece[...]
-    square = arrived[0, :, width : width + LANES]
-    begin = arrived[0, :, width + LANES :]
+    for x, send in enumerate(sends):
+        high = send.shape[0] - 1
+        for y in range(high):
+            g = y * span + x
+            send[y] = panel[:, g * width : (g + 1) * width]
+        send[high, :, :LANES] = picked[...]
+        send[high, :, LANES:] = heads
+
+
+def relay_kernel(top, root, kept, *refs):
+    del top
+    others, out = refs[:-1], refs[-1]
+    for n in range(out.shape[0]):
+        total = jnp.where(root[0] == 1, kept[n], 0.0)
+        for other in others:
+            total = total + other[n]
+        out[n] = total
+
+
+def own_kernel(top, base, wanted, owned, block, out):
+    step = pl.program_id(0)
+
+    @pl.when(step == 0)
+    def _():
+        lanes = iota((block.shape[0], LANES), 1)
+        out[:, :LANES] = jnp.zeros(lanes.shape, F32)
+        out[:, LANES:] = jnp.where((base[0] == 0) & (lanes < top), block[:, :LANES], 0.0)
+
+    pick_rows(wanted, owned, base[0] + step * block.shape[1], block, out)
+
+
+def arrive_kernel(top, *refs):
+    del top
+    arrivals, (share, square) = refs[:-2], refs[-2:]
+    count = share.shape[0]
+    for n in range(count + 1):
+        total = arrivals[0][n]
+        for arrival in arrivals[1:]:
+            total = total + arrival[n]
+        if n < count:
+            share[n] = total
+        else:
+            square[...] = total
+
+
+def order_kernel(top, place, *refs):
+    del top
+    pieces, out = refs[:-1], refs[-1]
+    span = len(pieces)
+    for k, piece in enumerate(pieces):
+        owner = (place[0] + span - k) % span
+        for n in range(piece.shape[0]):
+            out[n * span + owner] = piece[n]
+
+
+def gather_kernel(top, pieces, panel_top, packed):
+    depth = pieces.shape[0]
+    square, begin = panel_top[:, :LANES], panel_top[:, LANES:]
+    total = pieces[0]
+    for z in range(1, depth):
+        total = total + pieces[z]
     third = LANES - top
     tail = iota(square.shape, 1) >= top
     for n, body in enumerate((total[:, :LANES], total[:, LANES:], square)):
         moved = pltpu.roll(begin, top - n * third, 1)
-        packed[:, n * LANES : (n + 1) * LANES] = jnp.where(tail, moved, body)
-
-
-def heads_kernel(top, place, *refs):
-    pieces, (heads, square) = refs[:-2], refs[-2:]
-    depth = len(pieces)
-    part = pieces[0].shape[0]
+        value = jnp.where(tail, moved, body)
+        for z in range(depth):
+            packed[z, :, n * LANES : (n + 1) * LANES] = value
+
+
+def heads_kernel(top, pieces, heads, square):
+    depth, part, _ = pieces.shape
     third = LANES - top
     lanes = iota((part, LANES), 1)
-    total = pieces[0][...]
-    for piece in pieces[1:]:
-        total = total + piece[...]
+    total = pieces[0]
+    for z in range(1, depth):
+        total = total + pieces[z]
     square[:, :LANES] = jnp.where(lanes < top, total[:, 2 * LANES :], 0.0)
     begin = jnp.zeros((part, LANES), F32)
     for n in range(3):
@@ -141,10 +175,8 @@
         begin = jnp.where((lanes >= n * third) & (lanes < (n + 1) * third), moved, begin)
     square[:, LANES:] = begin
     keep = iota((part, 2 * LANES), 1) % LANES < top
-    for k, piece in enumerate(pieces):
-        owner = (place[0] + depth - k) % depth
-        at = pl.ds(pl.multiple_of(owner * part, 8), part)
-        heads[at, :] = jnp.where(keep, piece[:, : 2 * LANES], 0.0)
+    for z in range(depth):
+        heads[z * part : (z + 1) * part, :] = jnp.where(keep, pieces[z, :, : 2 * LANES], 0.0)
 
 
 def spread(tile, j):
@@ -237,7 +269,7 @@
 
 def update_kernel(
     top, flags, heads, factor, lower_inv, upper_inv, starts, dest, block, mine, other, out,
-    lhs_a, lhs_b, lhs_c, top_out,
+    lhs, top_out,
 ):
     step = pl.program_id(0)
     half = mine.shape[1]
@@ -262,15 +294,10 @@
         )
         moved = begin - jnp.dot(weight, starts[...], precision=HI, preferred_element_type=F32)
         w_hi, w_lo = split(-weight)
-        z_hi = moved.astype(BF16)
-        left = moved - z_hi.astype(F32)
-        z_mid, z_lo = split(left)
-        lhs_a[:, :LANES] = w_hi
-        lhs_a[:, LANES:] = z_hi
-        lhs_b[:, :LANES] = w_lo
-        lhs_b[:, LANES:] = z_mid
-        lhs_c[:, :LANES] = w_hi
-        lhs_c[:, LANES:] = z_lo
+        z_hi, z_lo = split(moved)
+        parts = [p[:, :top] for p in (w_hi, w_lo, w_hi, z_hi, z_lo)]
+        parts.append(jnp.zeros((moved.shape[0], lhs.shape[1] - 5 * top), BF16))
+        lhs[...] = jnp.concatenate(parts, axis=1)
 
     groups = mine.shape[0]
     for g in range(groups):
@@ -278,18 +305,15 @@
         cols = slice(g * w, (g + 1) * w)
         m, o = mine[g], other[g]
         panel = jnp.concatenate([jnp.where(core == 0, m, o), jnp.where(core == 0, o, m)], axis=0)
-        where_to = jnp.concatenate([dest[...]] * (w // LANES), axis=1)
-        place = base + step * width + g * w + iota((LANES, w), 1)
+        where_to = jnp.concatenate([dest[:top, :]] * (w // LANES), axis=1)
+        place = base + step * width + g * w + iota((top, w), 1)
         hot = jnp.where(where_to == place, 1.0, 0.0)
         keep = 1.0 - jnp.sum(hot, axis=0, keepdims=True)
         p_hi, p_lo = split(panel * keep)
         hot = hot.astype(BF16)
-        fill = jnp.zeros((LANES - 2 * half, w), BF16)
-        rhs_a = jnp.concatenate([p_hi, fill, hot], axis=0)
-        rhs_c = jnp.concatenate([p_lo, fill, hot], axis=0)
-        acc = jnp.dot(lhs_a[...], rhs_a, preferred_element_type=F32)
-        acc += jnp.dot(lhs_b[...], rhs_a, preferred_element_type=F32)
-        acc += jnp.dot(lhs_c[...], rhs_c, preferred_element_type=F32)
+        fill = jnp.zeros((lhs.shape[1] - 5 * top, w), BF16)
+        rhs = jnp.concatenate([p_hi, p_hi, p_lo, hot, hot, fill], axis=0)
+        acc = jnp.dot(lhs[...], rhs, preferred_element_type=F32)
         keep_root = jnp.where(root == 1, 0.0, keep)
         out[:half, cols] = block[:half, cols] * keep_root + acc[:half]
         out[half:, cols] = block[half:, cols] * keep + acc[half:]
@@ -315,9 +339,6 @@
     base1 = base.reshape(1)
     swap = [(0, 1), (1, 0)]
 
-    def around(step):
-        return [(z, (z + step) % depth) for z in range(depth)]
-
     def call(kernel, name, us, out_shape, in_specs, out_specs, *args, **more):
         return pl.pallas_call(
             lambda *refs: kernel(top, *refs),
@@ -330,17 +351,20 @@
             **more,
         )(*args)
 
-    blocks16, wanted, dest = call(
+    span_x, span_y = lax.axis_size("x"), lax.axis_size("y")
+    send = jax.ShapeDtypeStruct((span_y + 1, half, width), F32)
+    *sends, wanted, owned, dest = call(
         start_kernel,
         "start",
         5,
         (
-            jax.ShapeDtypeStruct((chips, half, width + 2 * LANES), F32),
+            *[send] * span_x,
             jax.ShapeDtypeStruct((top,), jnp.int32),
+            jax.ShapeDtypeStruct((top + 8,), jnp.int32),
             jax.ShapeDtypeStruct((LANES, LANES), jnp.int32),
         ),
         [smem_spec(), smem_spec(), pl.BlockSpec((half, rows), lambda i: (0, 0))],
-        (vmem_spec(), smem_spec(), vmem_spec()),
+        (*[vmem_spec()] * span_x, smem_spec(), smem_spec(), vmem_spec()),
         pivots,
         base1,
         holdings,
@@ -351,39 +375,74 @@
             pltpu.VMEM((half, LANES), F32),
         ],
     )
-    arrived = lax.all_to_all(blocks16, plane, 0, 0)
-    piece = jax.ShapeDtypeStruct((cols // depth, 2 * LANES), F32)
+    along_x = [lax.ppermute(sends[k], plane, [(0, k)]) for k in range(1, span_x)]
     offered = call(
         own_kernel,
         "own",
         5,
-        (piece,) * depth,
-        [smem_spec(), smem_spec(), vmem_spec()],
-        (vmem_spec(),) * depth,
+        jax.ShapeDtypeStruct((cols, 2 * LANES), F32),
+        [smem_spec()] * 3 + [pl.BlockSpec((cols, rows // 2), lambda i: (0, i))],
+        pl.BlockSpec((cols, 2 * LANES), lambda i: (0, 0)),
         base1,
         wanted,
+        owned,
         holdings,
-        scratch_shapes=[pltpu.VMEM((cols, LANES), F32)],
-    )
-    pieces = [offered[0]]
-    pieces += [lax.ppermute(offered[k], "prow", around(k)) for k in range(1, depth)]
-    shares, packed = call(
+        grid=(2,),
+    )
+    relayed = call(
+        relay_kernel,
+        "relay",
+        1,
+        send,
+        [smem_spec()] + [vmem_spec()] * span_x,
+        vmem_spec(),
+        root.reshape(1),
+        sends[0],
+        *along_x,
+    )
+    offered, relayed = lax.optimization_barrier((offered, relayed))
+    along_y = [
+        lax.ppermute(relayed, plane, [(x, k * span_x + x) for x in range(span_x)])
+        for k in range(1, span_y)
+    ]
+    share, panel_top = call(
+        arrive_kernel,
+        "arrive",
+        0.5,
+        (jax.ShapeDtypeStruct((span_y, half, width), F32), jax.ShapeDtypeStruct((half, width), F32)),
+        [vmem_spec()] * span_y,
+        (vmem_spec(), vmem_spec()),
+        relayed,
+        *along_y,
+    )
+
+    part = cols // depth
+    pieces = lax.all_to_all(offered.reshape(depth, part, 2 * LANES), "prow", 0, 0)
+    packed = call(
         gather_kernel,
         "gather",
-        2,
-        (
-            jax.ShapeDtypeStruct((chips, half, width), F32),
-            jax.ShapeDtypeStruct((half, 3 * LANES), F32),
-        ),
-        [pl.BlockSpec((1, half, width + 2 * LANES), lambda i: (0, 0, 0))]
-        + [pl.BlockSpec(piece.shape, lambda i: (0, 0))] * depth,
-        (vmem_spec(), vmem_spec()),
-        arrived,
-        *pieces,
-        grid=(1,),
-    )
-    mine = lax.all_to_all(shares, plane, 0, 0)
-    slices = [packed] + [lax.ppermute(packed, "prow", around(k)) for k in range(1, depth)]
+        1,
+        jax.ShapeDtypeStruct((depth, part, 3 * LANES), F32),
+        [vmem_spec(), vmem_spec()],
+        vmem_spec(),
+        pieces,
+        panel_top,
+    )
+    packed, share = lax.optimization_barrier((packed, share))
+    found = [share]
+    for k in range(1, span_x):
+        moves = [(i, (i + k) % span_x) for i in range(span_x)]
+        found.append(lax.ppermute(share, "x", moves))
+    mine = call(
+        order_kernel,
+        "order",
+        0.7,
+        jax.ShapeDtypeStruct((chips, half, width), F32),
+        [smem_spec()] + [vmem_spec()] * span_x,
+        vmem_spec(),
+        lax.axis_index("x").astype(jnp.int32).reshape(1),
+        *found,
+    )
     heads, square = call(
         heads_kernel,
         "heads",
@@ -392,10 +451,9 @@
             jax.ShapeDtypeStruct((cols, 2 * LANES), F32),
             jax.ShapeDtypeStruct((half, 2 * LANES), F32),
         ),
-        [smem_spec()] + [vmem_spec()] * depth,
+        [vmem_spec()],
         (vmem_spec(), vmem_spec()),
-        base1 // rows,
-        *slices,
+        lax.all_to_all(packed, "prow", 0, 0),
     )
     square_other = lax.ppermute(square, "core", swap)
     mine, square_other = lax.optimization_barrier((mine, square_other))
@@ -411,7 +469,7 @@
         name="factor",
     )(core.reshape(1), square, square_other)
     flags = jnp.stack([core, root, base])
-    per_step = 4
+    per_step = 8
     span = per_step * width
     whole = pl.BlockSpec((LANES, LANES), lambda i: (0, 0))
     parts = pl.BlockSpec((per_step, half, width), lambda i: (i, 0, 0))
@@ -433,9 +491,7 @@
         ],
         out_specs=pl.BlockSpec((cols, span), lambda i: (0, i)),
         scratch_shapes=[
-            pltpu.VMEM((cols, 2 * LANES), BF16),
-            pltpu.VMEM((cols, 2 * LANES), BF16),
-            pltpu.VMEM((cols, 2 * LANES), BF16),
+            pltpu.VMEM((cols, 4 * LANES), BF16),
             pltpu.VMEM((cols, LANES), F32),
         ],
         compiler_params=params(),

time: 88.2 us -> 80.5 us (0.913)
  starting transfers between devices: 43.1 us -> 33.5 us
  waiting for transfers between devices: 16.1 us -> 22.4 us
  Pallas kernels: 27.2 us -> 22.3 us
    all_to_all x2, waiting for transfers between devices: 0.01 us -> 12.3 us  [the longest x1 11.6 us: on_device(): lax.all_to_all(packed, 'prow', 0, 0)]
    ppermute x14 -> x9, starting transfers between devices: 26.4 us -> 15.9 us  [the longest x3 7.47 us: on_device(): lax.ppermute(sends[k], plane, [(0, k)])]
    ppermute x14 -> x9, waiting for transfers between devices: 15.2 us -> 9.22 us  [the longest x3 7.62 us: on_device(): lax.ppermute(relayed, plane, [(x, k * span_x + x) for x in range(span_x)])]
    pallas_call x4 -> x7, Pallas kernels: 12.9 us -> 9.86 us  [call(): pl.pallas_call(lambda *refs: kernel(top, *refs), out_shape=out_shape, in_...]
    pallas_call x1, Pallas kernels: 8.69 us -> 6.9 us  [on_device(): pl.pallas_call(lambda *refs: update_kernel(top, *refs), grid=(rows // spa...]
  transfers between devices with their start and end apart: 18 -> 13, of which waited for: 7 -> 7; matrix products, arithmetic and copies ran while one was open for 0% -> 0% of each run, Pallas kernels for 14% -> 13%
where the time goes in v2:
time: 80.5 us; the launch traced here: 79 us
  starting transfers between devices  33.5 us (42%)
  waiting for transfers between devices  22.4 us (28%)
  Pallas kernels  22.3 us (28%)
    all_to_all x1, waiting for transfers between devices, on_device(): lax.all_to_all(packed, 'prow', 0, 0)  11.6 us
    pallas_call x7, Pallas kernels, call(): pl.pallas_call(lambda *refs: kernel(top, *refs), out_shape=out_shape, in_...  9.86 us
    all_to_all x1, starting transfers between devices, on_device(): lax.all_to_all(offered.reshape(depth, part, 2 * LANES), 'prow', 0, 0)  7.79 us
    ppermute x3, waiting for transfers between devices, on_device(): lax.ppermute(relayed, plane, [(x, k * span_x + x) for x in range(span_x)])  7.62 us
    ppermute x3, starting transfers between devices, on_device(): lax.ppermute(sends[k], plane, [(0, k)])  7.47 us
    pallas_call x1, Pallas kernels, on_device(): pl.pallas_call(lambda *refs: update_kernel(top, *refs), grid=(rows // spa...  6.9 us
    all_to_all x1, starting transfers between devices, on_device(): lax.all_to_all(packed, 'prow', 0, 0)  5.62 us
    pallas_call x1, Pallas kernels, on_device(): pl.pallas_call(factor_kernel, out_shape=(small,) * 4, in_specs=[smem_spec...  5.55 us
  transfers between devices with their start and end apart: 13, of which 7 were waited for; matrix products, arithmetic and copies ran while one was open for 0% of the time, Pallas kernels for 13%

profile of v2, /device:TPU:1, one launch (start us, length us, event | category | flops | bytes accessed | tf_op | source)
XLA Modules:
  0.0 79.0 jit_solution(16378525741443749641)
XLA Ops:
  0.0 0.7 copy-done
  0.7 3.9 %start.1 = (f32[5,48,256]{2,1,0:T(8,128)S(1)}, f32[5,48,256]{2,1,0:T(8,128)S(1)}, f32[5,48,256]{2,1,0:T(8,128)S(1)}, f32[5,48,256]{2,1,0:T(8,128)S(1)}, s32[96]{...) custom-call(s32[96]{0:T(128)S(1)} %copy-done, s32[1]{0:T(128)} %bitcast.2.refs_1_.refs_0_, f32[384,4096]{1,0:T(8,128)} %bitcast.9), custom_call_target="tpu_custom_call" | custom-call | bytes 17500000 | tf_op jit(solution)/shard_map/start/pallas_call | solution.py:343
  4.6 4.0 %collective-permute-start = (f32[5,48,256]{2,1,0:T(8,128)S(1)}, f32[5,48,256]{2,1,0:T(8,128)S(1)}, u32[]{:S(2)}, u32[]{:S(2)}) collective-permute-start(f32[5,48,256]{2,1,0:T(8,128)S(1)} %get-tuple-element.29), channel_id=1, source_target_pairs={{0,16},{1,17},{2,18},{3,19},{4,20},{5,21},{6,22},{7,23},{8,24},{9,... | collective-permute-start | bytes 737288 | tf_op jit(solution)/shard_map/ppermute | solution.py:378
  8.6 2.2 %collective-permute-start.1 = (f32[5,48,256]{2,1,0:T(8,128)S(1)}, f32[5,48,256]{2,1,0:T(8,128)S(1)}, u32[]{:S(2)}, u32[]{:S(2)}) collective-permute-start(f32[5,48,256]{2,1,0:T(8,128)S(1)} %get-tuple-element.30), channel_id=1, source_target_pairs={{0,32},{1,33},{2,34},{3,35},{4,36},{5,37},{6,38},{7,39},{8,40},{9,... | collective-permute-start | bytes 737288 | tf_op jit(solution)/shard_map/ppermute | solution.py:378
  10.8 1.3 %collective-permute-start.2 = (f32[5,48,256]{2,1,0:T(8,128)S(1)}, f32[5,48,256]{2,1,0:T(8,128)S(1)}, u32[]{:S(2)}, u32[]{:S(2)}) collective-permute-start(f32[5,48,256]{2,1,0:T(8,128)S(1)} %get-tuple-element.31), channel_id=1, source_target_pairs={{0,48},{1,49},{2,50},{3,51},{4,52},{5,53},{6,54},{7,55},{8,56},{9,... | collective-permute-start | bytes 737288 | tf_op jit(solution)/shard_map/ppermute | solution.py:378
  12.1 4.7 %own.1 = f32[384,256]{1,0:T(8,128)} custom-call(s32[1]{0:T(128)} %bitcast.2.refs_1_.refs_0_, s32[96]{0:T(128)S(1)} %get-tuple-element.26.refs_1_, s32[104]{0:T(128)S(1)} %get-tuple-element.27.refs_2_, f32[384,4096]{1,0:T(8,128)} %bitcast.10), custom_call_target="tpu_custom_call" | custom-call | bytes 17500000 | tf_op jit(solution)/shard_map/own/pallas_call | solution.py:343
  16.8 0.0 collective-permute-done.refs_2_
  16.8 1.6 %collective-permute-done.1.refs_3_ = f32[5,48,256]{2,1,0:T(8,128)S(1)} collective-permute-done((f32[5,48,256]{2,1,0:T(8,128)S(1)}, f32[5,48,256]{2,1,0:T(8,128)S(1)}, u32[]{:S(2)}, u32[]{:S(2)}) %collective-permute-start.1) | collective-permute-done | bytes 245792 | tf_op jit(solution)/shard_map/ppermute | solution.py:378
  18.4 0.0 collective-permute-done.2.refs_4_
  18.4 0.1 relay.1.refs_0_
  18.5 7.8 %all-to-all-start = ((f32[8,48,256]{2,1,0:T(8,128)}), f32[8,48,256]{2,1,0:T(8,128)S(1)}, u32[]{:S(2)}, u32[]{:S(2)}) async-start(f32[8,48,256]{2,1,0:T(8,128)} %bitcast.4), calls=%async_computation | async-start | bytes 786432 | tf_op jit(solution)/shard_map/all_to_all | solution.py:420
  26.3 1.3 %collective-permute-start.5 = (f32[5,48,256]{2,1,0:T(8,128)S(1)}, f32[5,48,256]{2,1,0:T(8,128)S(1)}, u32[]{:S(2)}, u32[]{:S(2)}) collective-permute-start(f32[5,48,256]{2,1,0:T(8,128)S(1)} %relay.1.refs_0_), channel_id=1, source_target_pairs={{0,192},{16,208},{32,224},{48,240},{1,193},{17,209},{33,225},{49,2... | collective-permute-start | bytes 737288 | tf_op jit(solution)/shard_map/ppermute | solution.py:405
  27.6 1.3 %collective-permute-start.4 = (f32[5,48,256]{2,1,0:T(8,128)S(1)}, f32[5,48,256]{2,1,0:T(8,128)S(1)}, u32[]{:S(2)}, u32[]{:S(2)}) collective-permute-start(f32[5,48,256]{2,1,0:T(8,128)S(1)} %relay.1.refs_0_), channel_id=1, source_target_pairs={{0,128},{16,144},{32,160},{48,176},{1,129},{17,145},{33,161},{49,1... | collective-permute-start | bytes 737288 | tf_op jit(solution)/shard_map/ppermute | solution.py:405
  28.9 1.3 %collective-permute-start.3 = (f32[5,48,256]{2,1,0:T(8,128)S(1)}, f32[5,48,256]{2,1,0:T(8,128)S(1)}, u32[]{:S(2)}, u32[]{:S(2)}) collective-permute-start(f32[5,48,256]{2,1,0:T(8,128)S(1)} %relay.1.refs_0_), channel_id=1, source_target_pairs={{0,64},{16,80},{32,96},{48,112},{1,65},{17,81},{33,97},{49,113},{2... | collective-permute-start | bytes 737288 | tf_op jit(solution)/shard_map/ppermute | solution.py:405
  30.2 1.0 %collective-permute-done.5.refs_3_ = f32[5,48,256]{2,1,0:T(8,128)S(1)} collective-permute-done((f32[5,48,256]{2,1,0:T(8,128)S(1)}, f32[5,48,256]{2,1,0:T(8,128)S(1)}, u32[]{:S(2)}, u32[]{:S(2)}) %collective-permute-start.5) | collective-permute-done | bytes 245792 | tf_op jit(solution)/shard_map/ppermute | solution.py:405
  31.3 1.3 %collective-permute-done.4.refs_2_ = f32[5,48,256]{2,1,0:T(8,128)S(1)} collective-permute-done((f32[5,48,256]{2,1,0:T(8,128)S(1)}, f32[5,48,256]{2,1,0:T(8,128)S(1)}, u32[]{:S(2)}, u32[]{:S(2)}) %collective-permute-start.4) | collective-permute-done | bytes 245792 | tf_op jit(solution)/shard_map/ppermute | solution.py:405
  32.6 5.3 %collective-permute-done.3.refs_1_ = f32[5,48,256]{2,1,0:T(8,128)S(1)} collective-permute-done((f32[5,48,256]{2,1,0:T(8,128)S(1)}, f32[5,48,256]{2,1,0:T(8,128)S(1)}, u32[]{:S(2)}, u32[]{:S(2)}) %collective-permute-start.3) | collective-permute-done | bytes 245792 | tf_op jit(solution)/shard_map/ppermute | solution.py:405
  37.9 0.8 all-to-all-done.refs_0_
  38.6 0.9 %gather.1 = f32[8,48,384]{2,1,0:T(8,128)} custom-call(f32[8,48,256]{2,1,0:T(8,128)S(1)} %all-to-all-done.refs_0_, f32[48,256]{1,0:T(8,128)S(1)} %get-tuple-element.34.refs_1_), custom_call_target="tpu_custom_call" | custom-call | bytes 3500000 | tf_op jit(solution)/shard_map/gather/pallas_call | solution.py:343
  39.6 5.6 %all-to-all-start.1 = ((f32[8,48,384]{2,1,0:T(8,128)}), f32[8,48,384]{2,1,0:T(8,128)S(1)}, u32[]{:S(2)}, u32[]{:S(2)}) async-start(f32[8,48,384]{2,1,0:T(8,128)} %gather.1), calls=%async_computation.1 | async-start | bytes 1179648 | tf_op jit(solution)/shard_map/all_to_all | solution.py:456
  45.2 1.7 %collective-permute-start.8 = (f32[4,48,256]{2,1,0:T(8,128)S(1)}, f32[4,48,256]{2,1,0:T(8,128)S(1)}, u32[]{:S(2)}, u32[]{:S(2)}) collective-permute-start(f32[4,48,256]{2,1,0:T(8,128)S(1)} %get-tuple-element.39.refs_1_), channel_id=1, source_target_pairs={{0,48},{16,0},{32,16},{48,32},{1,49},{17,1},{33,17},{49,33},{2,50}... | collective-permute-start | bytes 589832 | tf_op jit(solution)/shard_map/ppermute | solution.py:435
  46.9 2.1 %collective-permute-start.7 = (f32[4,48,256]{2,1,0:T(8,128)S(1)}, f32[4,48,256]{2,1,0:T(8,128)S(1)}, u32[]{:S(2)}, u32[]{:S(2)}) collective-permute-start(f32[4,48,256]{2,1,0:T(8,128)S(1)} %get-tuple-element.39.refs_1_), channel_id=1, source_target_pairs={{0,32},{16,48},{32,0},{48,16},{1,33},{17,49},{33,1},{49,17},{2,34}... | collective-permute-start | bytes 589832 | tf_op jit(solution)/shard_map/ppermute | solution.py:435
  49.0 0.8 collective-permute-start.6
  49.8 11.6 %all-to-all-done.1.refs_0_ = f32[8,48,384]{2,1,0:T(8,128)S(1)} async-done(((f32[8,48,384]{2,1,0:T(8,128)}), f32[8,48,384]{2,1,0:T(8,128)S(1)}, u32[]{:S(2)}, u32[]{:S(2)}) %all-to-all-start.1) | async-done | bytes 589856 | tf_op jit(solution)/shard_map/all_to_all | solution.py:456
  61.3 0.1 heads.1
  61.4 3.8 %collective-permute-start.9 = (f32[48,256]{1,0:T(8,128)S(1)}, f32[48,256]{1,0:T(8,128)S(1)}, u32[]{:S(2)}, u32[]{:S(2)}) collective-permute-start(f32[48,256]{1,0:T(8,128)S(1)} %get-tuple-element.38.mine), channel_id=1, source_target_pairs={{0,8},{8,0},{1,9},{9,1},{2,10},{10,2},{3,11},{11,3},{4,12},{12,4},... | collective-permute-start | bytes 147464 | tf_op jit(solution)/shard_map/ppermute | solution.py:458
  65.2 0.1 order.1.refs_8_
  65.3 0.8 %collective-permute-done.9.other = f32[48,256]{1,0:T(8,128)S(1)} collective-permute-done((f32[48,256]{1,0:T(8,128)S(1)}, f32[48,256]{1,0:T(8,128)S(1)}, u32[]{:S(2)}, u32[]{:S(2)}) %collective-permute-start.9) | collective-permute-done | bytes 49184 | tf_op jit(solution)/shard_map/ppermute | solution.py:458
  66.1 0.3 collective-permute-start.10
  66.5 0.1 pad_add_fusion.refs_0_
  66.5 5.5 %factor.1 = (f32[128,128]{1,0:T(8,128)S(1)}, f32[128,128]{1,0:T(8,128)S(1)}, f32[128,128]{1,0:T(8,128)S(1)}, f32[128,128]{1,0:T(8,128)S(1)}) custom-call(s32[1]{0:T(128)} %bitcast.core, f32[48,256]{1,0:T(8,128)S(1)} %get-tuple-element.38.mine, f32[48,256]{1,0:T(8,128)S(1)} %collective-permute-done.9.other), custom_call_target="tpu_custom_call" | custom-call | bytes 31500000 | tf_op jit(solution)/shard_map/factor/pallas_call | solution.py:462
  72.1 6.9 %update.1 = f32[384,4096]{1,0:T(8,128)} custom-call(s32[3]{0:T(128)S(1)} %pad_add_fusion.refs_0_, f32[384,256]{1,0:T(8,128)S(1)} %get-tuple-element.37.refs_1_, f32[128,128]{1,0:T(8,128)S(1)} %get-tuple-element.41.refs_2_, f32[128,128]{1,0:T(8,128)S(1)} %get-tuple-element.42.refs_3_, f32[128,128]{1,0:T(8,128)S(1)} %get-tuple-element.43.refs_4_, ...), custom_call_target="tpu_custom_call" | custom-call | bytes 28000000 | tf_op jit(solution)/shard_map/update/pallas_call | solution.py:476
  (6 shorter events, 0.1 us)
Async XLA Ops:
  0.0 0.7 copy-start
  4.6 12.2 %collective-permute-start = (f32[5,48,256]{2,1,0:T(8,128)S(1)}, f32[5,48,256]{2,1,0:T(8,128)S(1)}, u32[]{:S(2)}, u32[]{:S(2)}) collective-permute-start(f32[5,48,256]{2,1,0:T(8,128)S(1)} %get-tuple-element.29), channel_id=1, source_target_pairs={{0,16},{1,17},{2,18},{3,19},{4,20},{5,21},{6,22},{7,23},{8,24},{9,... | collective-permute-start | bytes 737288 | tf_op jit(solution)/shard_map/ppermute | solution.py:378
  8.6 9.9 %collective-permute-start.1 = (f32[5,48,256]{2,1,0:T(8,128)S(1)}, f32[5,48,256]{2,1,0:T(8,128)S(1)}, u32[]{:S(2)}, u32[]{:S(2)}) collective-permute-start(f32[5,48,256]{2,1,0:T(8,128)S(1)} %get-tuple-element.30), channel_id=1, source_target_pairs={{0,32},{1,33},{2,34},{3,35},{4,36},{5,37},{6,38},{7,39},{8,40},{9,... | collective-permute-start | bytes 737288 | tf_op jit(solution)/shard_map/ppermute | solution.py:378
  10.8 7.6 %collective-permute-start.2 = (f32[5,48,256]{2,1,0:T(8,128)S(1)}, f32[5,48,256]{2,1,0:T(8,128)S(1)}, u32[]{:S(2)}, u32[]{:S(2)}) collective-permute-start(f32[5,48,256]{2,1,0:T(8,128)S(1)} %get-tuple-element.31), channel_id=1, source_target_pairs={{0,48},{1,49},{2,50},{3,51},{4,52},{5,53},{6,54},{7,55},{8,56},{9,... | collective-permute-start | bytes 737288 | tf_op jit(solution)/shard_map/ppermute | solution.py:378
  18.5 20.1 %all-to-all-start = ((f32[8,48,256]{2,1,0:T(8,128)}), f32[8,48,256]{2,1,0:T(8,128)S(1)}, u32[]{:S(2)}, u32[]{:S(2)}) async-start(f32[8,48,256]{2,1,0:T(8,128)} %bitcast.4), calls=%async_computation | async-start | bytes 786432 | tf_op jit(solution)/shard_map/all_to_all | solution.py:420
  26.3 5.0 %collective-permute-start.5 = (f32[5,48,256]{2,1,0:T(8,128)S(1)}, f32[5,48,256]{2,1,0:T(8,128)S(1)}, u32[]{:S(2)}, u32[]{:S(2)}) collective-permute-start(f32[5,48,256]{2,1,0:T(8,128)S(1)} %relay.1.refs_0_), channel_id=1, source_target_pairs={{0,192},{16,208},{32,224},{48,240},{1,193},{17,209},{33,225},{49,2... | collective-permute-start | bytes 737288 | tf_op jit(solution)/shard_map/ppermute | solution.py:405
  27.6 5.0 %collective-permute-start.4 = (f32[5,48,256]{2,1,0:T(8,128)S(1)}, f32[5,48,256]{2,1,0:T(8,128)S(1)}, u32[]{:S(2)}, u32[]{:S(2)}) collective-permute-start(f32[5,48,256]{2,1,0:T(8,128)S(1)} %relay.1.refs_0_), channel_id=1, source_target_pairs={{0,128},{16,144},{32,160},{48,176},{1,129},{17,145},{33,161},{49,1... | collective-permute-start | bytes 737288 | tf_op jit(solution)/shard_map/ppermute | solution.py:405
  28.9 8.9 %collective-permute-start.3 = (f32[5,48,256]{2,1,0:T(8,128)S(1)}, f32[5,48,256]{2,1,0:T(8,128)S(1)}, u32[]{:S(2)}, u32[]{:S(2)}) collective-permute-start(f32[5,48,256]{2,1,0:T(8,128)S(1)} %relay.1.refs_0_), channel_id=1, source_target_pairs={{0,64},{16,80},{32,96},{48,112},{1,65},{17,81},{33,97},{49,113},{2... | collective-permute-start | bytes 737288 | tf_op jit(solution)/shard_map/ppermute | solution.py:405
  39.6 21.8 %all-to-all-start.1 = ((f32[8,48,384]{2,1,0:T(8,128)}), f32[8,48,384]{2,1,0:T(8,128)S(1)}, u32[]{:S(2)}, u32[]{:S(2)}) async-start(f32[8,48,384]{2,1,0:T(8,128)} %gather.1), calls=%async_computation.1 | async-start | bytes 1179648 | tf_op jit(solution)/shard_map/all_to_all | solution.py:456
  45.2 20.0 %collective-permute-start.8 = (f32[4,48,256]{2,1,0:T(8,128)S(1)}, f32[4,48,256]{2,1,0:T(8,128)S(1)}, u32[]{:S(2)}, u32[]{:S(2)}) collective-permute-start(f32[4,48,256]{2,1,0:T(8,128)S(1)} %get-tuple-element.39.refs_1_), channel_id=1, source_target_pairs={{0,48},{16,0},{32,16},{48,32},{1,49},{17,1},{33,17},{49,33},{2,50}... | collective-permute-start | bytes 589832 | tf_op jit(solution)/shard_map/ppermute | solution.py:435
  46.9 18.4 %collective-permute-start.7 = (f32[4,48,256]{2,1,0:T(8,128)S(1)}, f32[4,48,256]{2,1,0:T(8,128)S(1)}, u32[]{:S(2)}, u32[]{:S(2)}) collective-permute-start(f32[4,48,256]{2,1,0:T(8,128)S(1)} %get-tuple-element.39.refs_1_), channel_id=1, source_target_pairs={{0,32},{16,48},{32,0},{48,16},{1,33},{17,49},{33,1},{49,17},{2,34}... | collective-permute-start | bytes 589832 | tf_op jit(solution)/shard_map/ppermute | solution.py:435
  49.0 16.3 %collective-permute-start.6 = (f32[4,48,256]{2,1,0:T(8,128)S(1)}, f32[4,48,256]{2,1,0:T(8,128)S(1)}, u32[]{:S(2)}, u32[]{:S(2)}) collective-permute-start(f32[4,48,256]{2,1,0:T(8,128)S(1)} %get-tuple-element.39.refs_1_), channel_id=1, source_target_pairs={{0,16},{16,32},{32,48},{48,0},{1,17},{17,33},{33,49},{49,1},{2,18}... | collective-permute-start | bytes 589832 | tf_op jit(solution)/shard_map/ppermute | solution.py:435
  61.4 4.7 %collective-permute-start.9 = (f32[48,256]{1,0:T(8,128)S(1)}, f32[48,256]{1,0:T(8,128)S(1)}, u32[]{:S(2)}, u32[]{:S(2)}) collective-permute-start(f32[48,256]{1,0:T(8,128)S(1)} %get-tuple-element.38.mine), channel_id=1, source_target_pairs={{0,8},{8,0},{1,9},{9,1},{2,10},{10,2},{3,11},{11,3},{4,12},{12,4},... | collective-permute-start | bytes 147464 | tf_op jit(solution)/shard_map/ppermute | solution.py:458
  66.1 6.0 %collective-permute-start.10 = (f32[16,48,256]{2,1,0:T(8,128)S(1)}, f32[16,48,256]{2,1,0:T(8,128)S(1)}, u32[]{:S(2)}, u32[]{:S(2)}) collective-permute-start(f32[16,48,256]{2,1,0:T(8,128)S(1)} %order.1.refs_8_), channel_id=1, source_target_pairs={{0,8},{8,0},{1,9},{9,1},{2,10},{10,2},{3,11},{11,3},{4,12},{12,4},... | collective-permute-start | bytes 2359304 | tf_op jit(solution)/shard_map/ppermute | solution.py:460

commit v3 on v2

--- a/solution.py
+++ b/solution.py
@@ -210,7 +210,7 @@
     square = jnp.concatenate(tiles + [rest], axis=0)
     lanes = iota((8, LANES), 1)
     subs = iota((8, LANES), 0)
-    ahead = 2
+    ahead = 5
     window = [[spread(t, q) for t in tiles] for q in range(ahead)]
     for j in range(extent):
         tj, sj = j // 8, j % 8

time: 80.5 us -> 78.5 us (0.975)
  Pallas kernels: 22.3 us -> 20.1 us
    pallas_call x1, Pallas kernels: 5.55 us -> 3.39 us  [on_device(): pl.pallas_call(factor_kernel, out_shape=(small,) * 4, in_specs=[smem_spec...]
  transfers between devices with their start and end apart: 13 -> 13, of which waited for: 7 -> 7; matrix products, arithmetic and copies ran while one was open for 0% -> 0% of each run, Pallas kernels for 13% -> 11%
where the time goes in v3:
time: 78.5 us; the launch traced here: 77 us
  starting transfers between devices  33.7 us (43%)
  waiting for transfers between devices  22.3 us (28%)
  Pallas kernels  20.1 us (26%)
    all_to_all x1, waiting for transfers between devices, on_device(): lax.all_to_all(packed, 'prow', 0, 0)  11.6 us
    pallas_call x7, Pallas kernels, call(): pl.pallas_call(lambda *refs: kernel(top, *refs), out_shape=out_shape, in_...  9.83 us
    all_to_all x1, starting transfers between devices, on_device(): lax.all_to_all(offered.reshape(depth, part, 2 * LANES), 'prow', 0, 0)  8 us
    ppermute x3, waiting for transfers between devices, on_device(): lax.ppermute(relayed, plane, [(x, k * span_x + x) for x in range(span_x)])  7.62 us
    ppermute x3, starting transfers between devices, on_device(): lax.ppermute(sends[k], plane, [(0, k)])  7.47 us
    pallas_call x1, Pallas kernels, on_device(): pl.pallas_call(lambda *refs: update_kernel(top, *refs), grid=(rows // spa...  6.9 us
    all_to_all x1, starting transfers between devices, on_device(): lax.all_to_all(packed, 'prow', 0, 0)  5.62 us
    ppermute x3, starting transfers between devices, on_device(): found.append(lax.ppermute(share, 'x', moves))  4.57 us
  transfers between devices with their start and end apart: 13, of which 7 were waited for; matrix products, arithmetic and copies ran while one was open for 0% of the time, Pallas kernels for 11%

profile of v3, /device:TPU:1, one launch (start us, length us, event | category | flops | bytes accessed | tf_op | source)
XLA Modules:
  0.0 77.0 jit_solution(12246907920907173475)
XLA Ops:
  0.0 0.7 copy-done
  0.7 3.9 %start.1 = (f32[5,48,256]{2,1,0:T(8,128)S(1)}, f32[5,48,256]{2,1,0:T(8,128)S(1)}, f32[5,48,256]{2,1,0:T(8,128)S(1)}, f32[5,48,256]{2,1,0:T(8,128)S(1)}, s32[96]{...) custom-call(s32[96]{0:T(128)S(1)} %copy-done, s32[1]{0:T(128)} %bitcast.2.refs_1_.refs_0_, f32[384,4096]{1,0:T(8,128)} %bitcast.9), custom_call_target="tpu_custom_call" | custom-call | bytes 17500000 | tf_op jit(solution)/shard_map/start/pallas_call | solution.py:343
  4.5 4.0 %collective-permute-start = (f32[5,48,256]{2,1,0:T(8,128)S(1)}, f32[5,48,256]{2,1,0:T(8,128)S(1)}, u32[]{:S(2)}, u32[]{:S(2)}) collective-permute-start(f32[5,48,256]{2,1,0:T(8,128)S(1)} %get-tuple-element.29), channel_id=1, source_target_pairs={{0,16},{1,17},{2,18},{3,19},{4,20},{5,21},{6,22},{7,23},{8,24},{9,... | collective-permute-start | bytes 737288 | tf_op jit(solution)/shard_map/ppermute | solution.py:378
  8.5 2.2 %collective-permute-start.1 = (f32[5,48,256]{2,1,0:T(8,128)S(1)}, f32[5,48,256]{2,1,0:T(8,128)S(1)}, u32[]{:S(2)}, u32[]{:S(2)}) collective-permute-start(f32[5,48,256]{2,1,0:T(8,128)S(1)} %get-tuple-element.30), channel_id=1, source_target_pairs={{0,32},{1,33},{2,34},{3,35},{4,36},{5,37},{6,38},{7,39},{8,40},{9,... | collective-permute-start | bytes 737288 | tf_op jit(solution)/shard_map/ppermute | solution.py:378
  10.7 1.3 %collective-permute-start.2 = (f32[5,48,256]{2,1,0:T(8,128)S(1)}, f32[5,48,256]{2,1,0:T(8,128)S(1)}, u32[]{:S(2)}, u32[]{:S(2)}) collective-permute-start(f32[5,48,256]{2,1,0:T(8,128)S(1)} %get-tuple-element.31), channel_id=1, source_target_pairs={{0,48},{1,49},{2,50},{3,51},{4,52},{5,53},{6,54},{7,55},{8,56},{9,... | collective-permute-start | bytes 737288 | tf_op jit(solution)/shard_map/ppermute | solution.py:378
  12.0 4.8 %own.1 = f32[384,256]{1,0:T(8,128)} custom-call(s32[1]{0:T(128)} %bitcast.2.refs_1_.refs_0_, s32[96]{0:T(128)S(1)} %get-tuple-element.26.refs_1_, s32[104]{0:T(128)S(1)} %get-tuple-element.27.refs_2_, f32[384,4096]{1,0:T(8,128)} %bitcast.10), custom_call_target="tpu_custom_call" | custom-call | bytes 17500000 | tf_op jit(solution)/shard_map/own/pallas_call | solution.py:343
  16.8 0.0 collective-permute-done.refs_2_
  16.8 1.5 %collective-permute-done.1.refs_3_ = f32[5,48,256]{2,1,0:T(8,128)S(1)} collective-permute-done((f32[5,48,256]{2,1,0:T(8,128)S(1)}, f32[5,48,256]{2,1,0:T(8,128)S(1)}, u32[]{:S(2)}, u32[]{:S(2)}) %collective-permute-start.1) | collective-permute-done | bytes 245792 | tf_op jit(solution)/shard_map/ppermute | solution.py:378
  18.4 0.0 collective-permute-done.2.refs_4_
  18.4 0.1 relay.1.refs_0_
  18.4 8.0 %all-to-all-start = ((f32[8,48,256]{2,1,0:T(8,128)}), f32[8,48,256]{2,1,0:T(8,128)S(1)}, u32[]{:S(2)}, u32[]{:S(2)}) async-start(f32[8,48,256]{2,1,0:T(8,128)} %bitcast.4), calls=%async_computation | async-start | bytes 786432 | tf_op jit(solution)/shard_map/all_to_all | solution.py:420
  26.4 1.3 %collective-permute-start.5 = (f32[5,48,256]{2,1,0:T(8,128)S(1)}, f32[5,48,256]{2,1,0:T(8,128)S(1)}, u32[]{:S(2)}, u32[]{:S(2)}) collective-permute-start(f32[5,48,256]{2,1,0:T(8,128)S(1)} %relay.1.refs_0_), channel_id=1, source_target_pairs={{0,192},{16,208},{32,224},{48,240},{1,193},{17,209},{33,225},{49,2... | collective-permute-start | bytes 737288 | tf_op jit(solution)/shard_map/ppermute | solution.py:405
  27.7 1.3 %collective-permute-start.4 = (f32[5,48,256]{2,1,0:T(8,128)S(1)}, f32[5,48,256]{2,1,0:T(8,128)S(1)}, u32[]{:S(2)}, u32[]{:S(2)}) collective-permute-start(f32[5,48,256]{2,1,0:T(8,128)S(1)} %relay.1.refs_0_), channel_id=1, source_target_pairs={{0,128},{16,144},{32,160},{48,176},{1,129},{17,145},{33,161},{49,1... | collective-permute-start | bytes 737288 | tf_op jit(solution)/shard_map/ppermute | solution.py:405
  29.0 1.3 %collective-permute-start.3 = (f32[5,48,256]{2,1,0:T(8,128)S(1)}, f32[5,48,256]{2,1,0:T(8,128)S(1)}, u32[]{:S(2)}, u32[]{:S(2)}) collective-permute-start(f32[5,48,256]{2,1,0:T(8,128)S(1)} %relay.1.refs_0_), channel_id=1, source_target_pairs={{0,64},{16,80},{32,96},{48,112},{1,65},{17,81},{33,97},{49,113},{2... | collective-permute-start | bytes 737288 | tf_op jit(solution)/shard_map/ppermute | solution.py:405
  30.3 1.0 %collective-permute-done.5.refs_3_ = f32[5,48,256]{2,1,0:T(8,128)S(1)} collective-permute-done((f32[5,48,256]{2,1,0:T(8,128)S(1)}, f32[5,48,256]{2,1,0:T(8,128)S(1)}, u32[]{:S(2)}, u32[]{:S(2)}) %collective-permute-start.5) | collective-permute-done | bytes 245792 | tf_op jit(solution)/shard_map/ppermute | solution.py:405
  31.4 1.3 %collective-permute-done.4.refs_2_ = f32[5,48,256]{2,1,0:T(8,128)S(1)} collective-permute-done((f32[5,48,256]{2,1,0:T(8,128)S(1)}, f32[5,48,256]{2,1,0:T(8,128)S(1)}, u32[]{:S(2)}, u32[]{:S(2)}) %collective-permute-start.4) | collective-permute-done | bytes 245792 | tf_op jit(solution)/shard_map/ppermute | solution.py:405
  32.7 5.3 %collective-permute-done.3.refs_1_ = f32[5,48,256]{2,1,0:T(8,128)S(1)} collective-permute-done((f32[5,48,256]{2,1,0:T(8,128)S(1)}, f32[5,48,256]{2,1,0:T(8,128)S(1)}, u32[]{:S(2)}, u32[]{:S(2)}) %collective-permute-start.3) | collective-permute-done | bytes 245792 | tf_op jit(solution)/shard_map/ppermute | solution.py:405
  38.0 0.8 all-to-all-done.refs_0_
  38.8 0.9 %gather.1 = f32[8,48,384]{2,1,0:T(8,128)} custom-call(f32[8,48,256]{2,1,0:T(8,128)S(1)} %all-to-all-done.refs_0_, f32[48,256]{1,0:T(8,128)S(1)} %get-tuple-element.34.refs_1_), custom_call_target="tpu_custom_call" | custom-call | bytes 3500000 | tf_op jit(solution)/shard_map/gather/pallas_call | solution.py:343
  39.7 5.6 %all-to-all-start.1 = ((f32[8,48,384]{2,1,0:T(8,128)}), f32[8,48,384]{2,1,0:T(8,128)S(1)}, u32[]{:S(2)}, u32[]{:S(2)}) async-start(f32[8,48,384]{2,1,0:T(8,128)} %gather.1), calls=%async_computation.1 | async-start | bytes 1179648 | tf_op jit(solution)/shard_map/all_to_all | solution.py:456
  45.3 1.7 %collective-permute-start.8 = (f32[4,48,256]{2,1,0:T(8,128)S(1)}, f32[4,48,256]{2,1,0:T(8,128)S(1)}, u32[]{:S(2)}, u32[]{:S(2)}) collective-permute-start(f32[4,48,256]{2,1,0:T(8,128)S(1)} %get-tuple-element.39.refs_1_), channel_id=1, source_target_pairs={{0,48},{16,0},{32,16},{48,32},{1,49},{17,1},{33,17},{49,33},{2,50}... | collective-permute-start | bytes 589832 | tf_op jit(solution)/shard_map/ppermute | solution.py:435
  47.0 2.1 %collective-permute-start.7 = (f32[4,48,256]{2,1,0:T(8,128)S(1)}, f32[4,48,256]{2,1,0:T(8,128)S(1)}, u32[]{:S(2)}, u32[]{:S(2)}) collective-permute-start(f32[4,48,256]{2,1,0:T(8,128)S(1)} %get-tuple-element.39.refs_1_), channel_id=1, source_target_pairs={{0,32},{16,48},{32,0},{48,16},{1,33},{17,49},{33,1},{49,17},{2,34}... | collective-permute-start | bytes 589832 | tf_op jit(solution)/shard_map/ppermute | solution.py:435
  49.1 0.8 collective-permute-start.6
  49.9 11.6 %all-to-all-done.1.refs_0_ = f32[8,48,384]{2,1,0:T(8,128)S(1)} async-done(((f32[8,48,384]{2,1,0:T(8,128)}), f32[8,48,384]{2,1,0:T(8,128)S(1)}, u32[]{:S(2)}, u32[]{:S(2)}) %all-to-all-start.1) | async-done | bytes 589856 | tf_op jit(solution)/shard_map/all_to_all | solution.py:456
  61.4 0.1 heads.1
  61.6 3.8 %collective-permute-start.9 = (f32[48,256]{1,0:T(8,128)S(1)}, f32[48,256]{1,0:T(8,128)S(1)}, u32[]{:S(2)}, u32[]{:S(2)}) collective-permute-start(f32[48,256]{1,0:T(8,128)S(1)} %get-tuple-element.38.mine), channel_id=1, source_target_pairs={{0,8},{8,0},{1,9},{9,1},{2,10},{10,2},{3,11},{11,3},{4,12},{12,4},... | collective-permute-start | bytes 147464 | tf_op jit(solution)/shard_map/ppermute | solution.py:458
  65.4 0.1 order.1.refs_8_
  65.4 0.8 %collective-permute-done.9.other = f32[48,256]{1,0:T(8,128)S(1)} collective-permute-done((f32[48,256]{1,0:T(8,128)S(1)}, f32[48,256]{1,0:T(8,128)S(1)}, u32[]{:S(2)}, u32[]{:S(2)}) %collective-permute-start.9) | collective-permute-done | bytes 49184 | tf_op jit(solution)/shard_map/ppermute | solution.py:458
  66.2 0.3 collective-permute-start.10
  66.6 0.1 pad_add_fusion.refs_0_
  66.7 3.4 %factor.1 = (f32[128,128]{1,0:T(8,128)S(1)}, f32[128,128]{1,0:T(8,128)S(1)}, f32[128,128]{1,0:T(8,128)S(1)}, f32[128,128]{1,0:T(8,128)S(1)}) custom-call(s32[1]{0:T(128)} %bitcast.core, f32[48,256]{1,0:T(8,128)S(1)} %get-tuple-element.38.mine, f32[48,256]{1,0:T(8,128)S(1)} %collective-permute-done.9.other), custom_call_target="tpu_custom_call" | custom-call | bytes 31500000 | tf_op jit(solution)/shard_map/factor/pallas_call | solution.py:462
  70.1 6.9 %update.1 = f32[384,4096]{1,0:T(8,128)} custom-call(s32[3]{0:T(128)S(1)} %pad_add_fusion.refs_0_, f32[384,256]{1,0:T(8,128)S(1)} %get-tuple-element.37.refs_1_, f32[128,128]{1,0:T(8,128)S(1)} %get-tuple-element.41.refs_2_, f32[128,128]{1,0:T(8,128)S(1)} %get-tuple-element.42.refs_3_, f32[128,128]{1,0:T(8,128)S(1)} %get-tuple-element.43.refs_4_, ...), custom_call_target="tpu_custom_call" | custom-call | bytes 28000000 | tf_op jit(solution)/shard_map/update/pallas_call | solution.py:476
  (6 shorter events, 0.1 us)
Async XLA Ops:
  0.0 0.7 copy-start
  4.5 12.3 %collective-permute-start = (f32[5,48,256]{2,1,0:T(8,128)S(1)}, f32[5,48,256]{2,1,0:T(8,128)S(1)}, u32[]{:S(2)}, u32[]{:S(2)}) collective-permute-start(f32[5,48,256]{2,1,0:T(8,128)S(1)} %get-tuple-element.29), channel_id=1, source_target_pairs={{0,16},{1,17},{2,18},{3,19},{4,20},{5,21},{6,22},{7,23},{8,24},{9,... | collective-permute-start | bytes 737288 | tf_op jit(solution)/shard_map/ppermute | solution.py:378
  8.5 9.9 %collective-permute-start.1 = (f32[5,48,256]{2,1,0:T(8,128)S(1)}, f32[5,48,256]{2,1,0:T(8,128)S(1)}, u32[]{:S(2)}, u32[]{:S(2)}) collective-permute-start(f32[5,48,256]{2,1,0:T(8,128)S(1)} %get-tuple-element.30), channel_id=1, source_target_pairs={{0,32},{1,33},{2,34},{3,35},{4,36},{5,37},{6,38},{7,39},{8,40},{9,... | collective-permute-start | bytes 737288 | tf_op jit(solution)/shard_map/ppermute | solution.py:378
  10.7 7.6 %collective-permute-start.2 = (f32[5,48,256]{2,1,0:T(8,128)S(1)}, f32[5,48,256]{2,1,0:T(8,128)S(1)}, u32[]{:S(2)}, u32[]{:S(2)}) collective-permute-start(f32[5,48,256]{2,1,0:T(8,128)S(1)} %get-tuple-element.31), channel_id=1, source_target_pairs={{0,48},{1,49},{2,50},{3,51},{4,52},{5,53},{6,54},{7,55},{8,56},{9,... | collective-permute-start | bytes 737288 | tf_op jit(solution)/shard_map/ppermute | solution.py:378
  18.4 20.4 %all-to-all-start = ((f32[8,48,256]{2,1,0:T(8,128)}), f32[8,48,256]{2,1,0:T(8,128)S(1)}, u32[]{:S(2)}, u32[]{:S(2)}) async-start(f32[8,48,256]{2,1,0:T(8,128)} %bitcast.4), calls=%async_computation | async-start | bytes 786432 | tf_op jit(solution)/shard_map/all_to_all | solution.py:420
  26.4 5.0 %collective-permute-start.5 = (f32[5,48,256]{2,1,0:T(8,128)S(1)}, f32[5,48,256]{2,1,0:T(8,128)S(1)}, u32[]{:S(2)}, u32[]{:S(2)}) collective-permute-start(f32[5,48,256]{2,1,0:T(8,128)S(1)} %relay.1.refs_0_), channel_id=1, source_target_pairs={{0,192},{16,208},{32,224},{48,240},{1,193},{17,209},{33,225},{49,2... | collective-permute-start | bytes 737288 | tf_op jit(solution)/shard_map/ppermute | solution.py:405
  27.7 5.0 %collective-permute-start.4 = (f32[5,48,256]{2,1,0:T(8,128)S(1)}, f32[5,48,256]{2,1,0:T(8,128)S(1)}, u32[]{:S(2)}, u32[]{:S(2)}) collective-permute-start(f32[5,48,256]{2,1,0:T(8,128)S(1)} %relay.1.refs_0_), channel_id=1, source_target_pairs={{0,128},{16,144},{32,160},{48,176},{1,129},{17,145},{33,161},{49,1... | collective-permute-start | bytes 737288 | tf_op jit(solution)/shard_map/ppermute | solution.py:405
  29.0 8.9 %collective-permute-start.3 = (f32[5,48,256]{2,1,0:T(8,128)S(1)}, f32[5,48,256]{2,1,0:T(8,128)S(1)}, u32[]{:S(2)}, u32[]{:S(2)}) collective-permute-start(f32[5,48,256]{2,1,0:T(8,128)S(1)} %relay.1.refs_0_), channel_id=1, source_target_pairs={{0,64},{16,80},{32,96},{48,112},{1,65},{17,81},{33,97},{49,113},{2... | collective-permute-start | bytes 737288 | tf_op jit(solution)/shard_map/ppermute | solution.py:405
  39.7 21.8 %all-to-all-start.1 = ((f32[8,48,384]{2,1,0:T(8,128)}), f32[8,48,384]{2,1,0:T(8,128)S(1)}, u32[]{:S(2)}, u32[]{:S(2)}) async-start(f32[8,48,384]{2,1,0:T(8,128)} %gather.1), calls=%async_computation.1 | async-start | bytes 1179648 | tf_op jit(solution)/shard_map/all_to_all | solution.py:456
  45.3 20.0 %collective-permute-start.8 = (f32[4,48,256]{2,1,0:T(8,128)S(1)}, f32[4,48,256]{2,1,0:T(8,128)S(1)}, u32[]{:S(2)}, u32[]{:S(2)}) collective-permute-start(f32[4,48,256]{2,1,0:T(8,128)S(1)} %get-tuple-element.39.refs_1_), channel_id=1, source_target_pairs={{0,48},{16,0},{32,16},{48,32},{1,49},{17,1},{33,17},{49,33},{2,50}... | collective-permute-start | bytes 589832 | tf_op jit(solution)/shard_map/ppermute | solution.py:435
  47.0 18.4 %collective-permute-start.7 = (f32[4,48,256]{2,1,0:T(8,128)S(1)}, f32[4,48,256]{2,1,0:T(8,128)S(1)}, u32[]{:S(2)}, u32[]{:S(2)}) collective-permute-start(f32[4,48,256]{2,1,0:T(8,128)S(1)} %get-tuple-element.39.refs_1_), channel_id=1, source_target_pairs={{0,32},{16,48},{32,0},{48,16},{1,33},{17,49},{33,1},{49,17},{2,34}... | collective-permute-start | bytes 589832 | tf_op jit(solution)/shard_map/ppermute | solution.py:435
  49.1 16.3 %collective-permute-start.6 = (f32[4,48,256]{2,1,0:T(8,128)S(1)}, f32[4,48,256]{2,1,0:T(8,128)S(1)}, u32[]{:S(2)}, u32[]{:S(2)}) collective-permute-start(f32[4,48,256]{2,1,0:T(8,128)S(1)} %get-tuple-element.39.refs_1_), channel_id=1, source_target_pairs={{0,16},{16,32},{32,48},{48,0},{1,17},{17,33},{33,49},{49,1},{2,18}... | collective-permute-start | bytes 589832 | tf_op jit(solution)/shard_map/ppermute | solution.py:435
  61.6 4.7 %collective-permute-start.9 = (f32[48,256]{1,0:T(8,128)S(1)}, f32[48,256]{1,0:T(8,128)S(1)}, u32[]{:S(2)}, u32[]{:S(2)}) collective-permute-start(f32[48,256]{1,0:T(8,128)S(1)} %get-tuple-element.38.mine), channel_id=1, source_target_pairs={{0,8},{8,0},{1,9},{9,1},{2,10},{10,2},{3,11},{11,3},{4,12},{12,4},... | collective-permute-start | bytes 147464 | tf_op jit(solution)/shard_map/ppermute | solution.py:458
  66.2 3.8 %collective-permute-start.10 = (f32[16,48,256]{2,1,0:T(8,128)S(1)}, f32[16,48,256]{2,1,0:T(8,128)S(1)}, u32[]{:S(2)}, u32[]{:S(2)}) collective-permute-start(f32[16,48,256]{2,1,0:T(8,128)S(1)} %order.1.refs_8_), channel_id=1, source_target_pairs={{0,8},{8,0},{1,9},{9,1},{2,10},{10,2},{3,11},{11,3},{4,12},{12,4},... | collective-permute-start | bytes 2359304 | tf_op jit(solution)/shard_map/ppermute | solution.py:460
